TPU v7x, 256 devices: a whole 4x4x8 slice. The times are simulated.
256 devices in a mesh: batch: 16 (over z_lo, x), tok: 8 (over y, z_hi), grp: 2 (over core).
Axes of the slice: x: 4, y: 4, z: 8 (z_hi: 2, z_lo: 4; z = z_hi * 4 + z_lo), core: 2. Of those that a mesh axis runs over, the one named last changes fastest.
Arguments:
- hidden: bfloat16 [32, 2048, 2432], P('batch', ('tok', 'grp')), may hold values from -6 to 6
- shift: float32 [32, 2432], P('batch'), may hold values from -3 to 3
- scale: float32 [32, 2432], P('batch'), may hold values from -3 to 3
- out_weight: bfloat16 [2432, 64], replicated, may hold values from -0.125 to 0.125
- noisy_latent: float32 [32, 64, 2048], P('batch', ('tok', 'grp')), may hold values from -16 to 16
- timestep: int32 [32], P('batch'), may hold values from 0 to 999
- in_kernel: bfloat16 [3, 3, 16, 512], replicated, may hold values from -0.5 to 0.5
- in_bias: float32 [512], replicated, may hold values from -4 to 4
- norm_gain: float32 [512], replicated, may hold values from 0.1 to 1.9
- norm_bias: float32 [512], replicated, may hold values from -3 to 3
- mid_kernel: bfloat16 [3, 3, 512, 512], replicated, may hold values from -0.09375 to 0.09375
- mid_bias: float32 [512], replicated, may hold values from -3 to 3
- rgb_weight: bfloat16 [512, 3], replicated, may hold values from -0.25 to 0.25
- clip_weight: bfloat16 [512, 1024], replicated, may hold values from -0.25 to 0.25
- text_embed: float32 [32, 1024], P('batch'), may hold values from -6 to 6
- slab_map: int32 [32, 16], P('batch', ('tok', 'grp')), may hold values from 0 to 15, each once within a row
Outputs:
- hidden_grad: bfloat16 [32, 2048, 2432], P('batch', ('tok', 'grp'))
- weight_grad: float32 [2432, 64], P(('batch', 'tok'))
- reward: float32 [32], P('batch')
- placed_pixels: float32 [32, 16, 4, 384], P('batch', ('tok', 'grp'))
Inputs may be any that keep to these rules, and one draw needn't show every extreme that they name: Each row of slab_map is a permutation of 0 to 15.
All inputs are finite; a program needn't handle non-finite values.
Results may differ from a plain program's by a relative error of at most 0.014.
Values may be sent and summed in bfloat16 or wider, within the bound.
A program may use at most 128 MiB of HBM per device.

v0:
```python
import jax
import jax.numpy as jnp
from jax import lax
from jax.sharding import PartitionSpec as P

LAT_CH = 16
VAE_CH = 512
GROUPS = 32


latent_scale = 1.5305
latent_shift = 0.0609
reward_weight = 16.0
epsilon = 1e-06


def extended(array, sides, width):
    for axis, dim in sides:
        devices, length = (lax.axis_size(axis), array.shape[dim])
        up = [(i, (i + 1) % devices) for i in range(devices - 1)]
        down = [(j, i) for i, j in up]
        last = lax.slice_in_dim(array, length - width, length, axis=dim)
        initial = lax.slice_in_dim(array, 0, width, axis=dim)
        before = lax.ppermute(last, axis, up)
        after = lax.ppermute(initial, axis, down)
        array = jnp.concatenate([before, array, after], axis=dim)
    return array


def noise_level(timestep):
    fraction = (timestep.astype(jnp.float32) + 1.0) / 1000.0
    return 3.0 * fraction / (1.0 + 2.0 * fraction)


def silu_slope(values):
    sigmoid = jax.nn.sigmoid(values)
    return sigmoid * (1.0 + values * (1.0 - sigmoid))


def convolve(padded, kernel):
    return lax.conv_general_dilated(
        padded,
        kernel,
        (1, 1),
        ((0, 0), (1, 1)),
        dimension_numbers=("NHWC", "HWIO", "NHWC"),
        preferred_element_type=jnp.float32,
    )


def transposed(kernel):
    return jnp.transpose(jnp.flip(kernel, (0, 1)), (0, 1, 3, 2))


def local(
    hidden,
    shift,
    scale,
    out_weight,
    noisy_latent,
    timestep,
    in_kernel,
    in_bias,
    norm_gain,
    norm_bias,
    mid_kernel,
    mid_bias,
    rgb_weight,
    clip_weight,
    text_embed,
    slab_map,
):
    images, tok_local, model_width = hidden.shape
    slab_rows = noisy_latent.shape[1]
    columns = noisy_latent.shape[2] // LAT_CH
    slabs = lax.axis_size(("tok", "grp"))
    cells = slab_rows * slabs * columns
    width_group = VAE_CH // GROUPS
    group_count = cells * width_group
    token_values = hidden.astype(jnp.float32)
    token_mean = jnp.mean(token_values, axis=-1, keepdims=True)
    centered = token_values - token_mean
    inverse_tok = lax.rsqrt(jnp.mean(centered * centered, axis=-1, keepdims=True) + epsilon)
    normalized_tok = centered * inverse_tok
    modulated = (
        (normalized_tok * (1.0 + scale[:, None, :]) + shift[:, None, :])
        .astype(jnp.bfloat16)
        .reshape(-1, model_width)
    )
    velocity = jnp.dot(modulated, out_weight, preferred_element_type=jnp.float32)
    velocity = (
        velocity.reshape(images, slab_rows // 2, columns // 2, 2, 2, LAT_CH)
        .transpose(0, 1, 3, 2, 4, 5)
        .reshape(images, slab_rows, columns * LAT_CH)
    )
    noise_sigma = noise_level(timestep)[:, None, None]
    latent = ((noisy_latent - noise_sigma * velocity) / latent_scale + latent_shift).astype(
        jnp.bfloat16
    )
    padded = extended(latent, ((("tok", "grp"), 1),), 1)
    first_out = (
        convolve(padded.reshape(images, slab_rows + 2, columns, LAT_CH), in_kernel) + in_bias
    )
    grouped = first_out.reshape(images, slab_rows * columns, GROUPS, width_group)
    group_sums, squares = lax.psum(
        (jnp.sum(grouped, axis=(1, 3)), jnp.sum(grouped * grouped, axis=(1, 3))), ("tok", "grp")
    )
    group_mean = group_sums / group_count
    inverse = lax.rsqrt(squares / group_count - group_mean * group_mean + epsilon)
    rows_here = first_out.shape[1]
    split = first_out.reshape(images, rows_here, columns, GROUPS, width_group)
    normalized = (
        (split - group_mean[:, None, None, :, None]) * inverse[:, None, None, :, None]
    ).reshape(first_out.shape)
    shaped = normalized * norm_gain + norm_bias
    act_one = jax.nn.silu(shaped).astype(jnp.bfloat16)
    act_ext = extended(act_one, ((("tok", "grp"), 1),), 1)
    second = convolve(act_ext, mid_kernel) + mid_bias
    act_two = jax.nn.silu(second)
    decoded = jnp.dot(
        act_two.astype(jnp.bfloat16).reshape(-1, VAE_CH),
        rgb_weight,
        preferred_element_type=jnp.float32,
    ).reshape(images, slab_rows, columns * 3)
    pooled = (lax.psum(jnp.sum(act_two, axis=(1, 2)), ("tok", "grp")) / cells).astype(jnp.bfloat16)
    feature = jnp.dot(pooled, clip_weight, preferred_element_type=jnp.float32)
    norm_feature = jnp.sqrt(jnp.sum(feature * feature, axis=-1, keepdims=True) + epsilon)
    norm_text = jnp.sqrt(jnp.sum(text_embed * text_embed, axis=-1, keepdims=True) + epsilon)
    reward = jnp.sum(feature * text_embed, axis=-1, keepdims=True) / (norm_feature * norm_text)
    grad_feature = (
        reward_weight
        * (
            text_embed / (norm_feature * norm_text)
            - reward * feature / (norm_feature * norm_feature)
        )
    ).astype(jnp.bfloat16)
    grad_act = jnp.dot(grad_feature, clip_weight.T, preferred_element_type=jnp.float32)
    grad_second = (grad_act[:, None, None, :] * silu_slope(second)).astype(jnp.bfloat16)
    grad_ext = extended(grad_second, ((("tok", "grp"), 1),), 1)
    grad_act_one = convolve(grad_ext, transposed(mid_kernel))
    scaled = grad_act_one * silu_slope(shaped) * norm_gain
    grouped_grad = scaled.reshape(images, slab_rows * columns, GROUPS, width_group)
    grouped_norm = normalized.reshape(images, slab_rows * columns, GROUPS, width_group)
    total_grad, total_cross = lax.psum(
        (jnp.sum(grouped_grad, axis=(1, 3)), jnp.sum(grouped_grad * grouped_norm, axis=(1, 3))),
        ("tok", "grp"),
    )
    grad_first = (
        grouped_grad
        - (total_grad / group_count)[:, None, :, None]
        - grouped_norm * (total_cross / group_count)[:, None, :, None]
    ) * inverse[:, None, :, None]
    grad_first = grad_first.reshape(images, slab_rows, columns, VAE_CH).astype(jnp.bfloat16)
    grad_first_ext = extended(grad_first, ((("tok", "grp"), 1),), 1)
    grad_latent = convolve(grad_first_ext, transposed(in_kernel)) / latent_scale
    grad_velocity = (
        (-noise_sigma[:, :, :, None] * grad_latent)
        .reshape(images, slab_rows // 2, 2, columns // 2, 2, LAT_CH)
        .transpose(0, 1, 3, 2, 4, 5)
    )
    grad_velocity = grad_velocity.reshape(images * tok_local, 4 * LAT_CH).astype(jnp.bfloat16)
    weight_term = jnp.dot(modulated.T, grad_velocity, preferred_element_type=jnp.float32) / (
        tok_local * slabs
    )
    paired = lax.psum(weight_term.astype(jnp.bfloat16), "grp").astype(jnp.float32)
    weight_grad = lax.psum_scatter(paired, ("batch", "tok"), scatter_dimension=0, tiled=True)
    grad_modulated = jnp.dot(
        grad_velocity, out_weight.T, preferred_element_type=jnp.float32
    ).reshape(images, tok_local, model_width)
    grad_normal = grad_modulated * (1.0 + scale[:, None, :])
    hidden_grad = (
        inverse_tok
        * (
            grad_normal
            - jnp.mean(grad_normal, axis=-1, keepdims=True)
            - normalized_tok * jnp.mean(grad_normal * normalized_tok, axis=-1, keepdims=True)
        )
    ).astype(jnp.bfloat16)
    gathered = lax.all_gather(decoded[:, None], ("tok", "grp"), axis=1, tiled=True)
    placed = jnp.take_along_axis(gathered, slab_map[:, :, None, None], axis=1)
    return (hidden_grad, weight_grad, reward[:, 0], placed)


def solution(mesh):
    return jax.shard_map(
        local,
        mesh=mesh,
        in_specs=(
            P("batch", ("tok", "grp"), None),
            P("batch", None),
            P("batch", None),
            P(),
            P("batch", ("tok", "grp"), None),
            P("batch"),
            P(),
            P(),
            P(),
            P(),
            P(),
            P(),
            P(),
            P(),
            P("batch", None),
            P("batch", ("tok", "grp")),
        ),
        out_specs=(
            P("batch", ("tok", "grp"), None),
            P(("batch", "tok"), None),
            P("batch"),
            P("batch", ("tok", "grp"), None, None),
        ),
        check_vma=False,
    )
```

profile of v0, /device:TPU:64, one launch (start us, length us, event | category | flops | bytes accessed | tf_op | source)
XLA Modules:
  0.0 1255.6 jit_solution(5758585684523236893)
XLA Ops:
  13.9 1.9 copy.177
  15.8 2.4 reshape.182
  20.4 2.3 collective-permute-start
  31.8 1.9 reshape.235
  37.2 1.9 reshape.183
  42.3 1.9 reshape.188
  45.4 2.0 fusion.39
  47.4 2.5 copy.180
  49.9 4.1 fusion.61
  56.5 3.1 copy.181
  62.2 52.5 %all-reduce.2 = (f32[2,32]{1,0:T(2,128)}, f32[2,32]{1,0:T(2,128)}) all-reduce(f32[2,32]{1,0:T(2,128)S(1)} %reduce_sum.140, f32[2,32]{1,0:T(2,128)S(1)} %reduce_sum.143), channel_id=1, replica_groups=mesh['batch'=16,'tok'=8,'grp'=2] {'tok','grp'}, use_global_device_ids=true, to_apply=%region_4.0 | all-reduce | flops 128 | bytes 1024 | tf_op jit(solution)/shard_map/psum | solution.py:105
  120.9 3.3 multiply_convert_fusion
  131.3 2.0 collective-permute-start.2
  133.3 1.9 copy.187
  149.1 7.5 fusion.53
  158.4 56.4 %psum.44 = f32[2,512]{1,0:T(2,128)S(1)} all-reduce(f32[2,512]{1,0:T(2,128)S(1)} %slice_reduce_fusion.2), channel_id=1, replica_groups=mesh['batch'=16,'tok'=8,'grp'=2] {'tok','grp'}, use_global_device_ids=true, to_apply=%region_9.10 | all-reduce | flops 1024 | bytes 8192 | tf_op jit(solution)/shard_map/psum | solution.py:125
  219.6 1.9 copy.195
  223.8 26.0 %all_gather.3 = f32[2,16,4,384]{3,2,0,1:T(4,128)} all-gather(f32[2,1,4,384]{3,2,0,1:T(4,128)S(1)} %broadcast_in_dim_reshape.3), channel_id=1, replica_groups=mesh['batch'=16,'tok'=8,'grp'=2] {'tok','grp'}, dimensions={1}, use_global_device_ids=true | all-gather | bytes 208896 | tf_op jit(solution)/shard_map/all_gather | solution.py:179
  253.4 2.9 collective-permute-start.4
  264.3 2.0 collective-permute-done.5
  266.3 2.9 maximum_bitcast_fusion.1
  272.3 1.9 fusion.23
  274.2 7.7 fusion.62
  283.8 3.1 copy.201
  287.3 58.2 %all-reduce.1 = (f32[2,32]{1,0:T(2,128)S(1)}, f32[2,32]{1,0:T(2,128)S(1)}) all-reduce(f32[2,32]{1,0:T(2,128)S(1)} %reduce_sum.153, f32[2,32]{1,0:T(2,128)S(1)} %reduce_sum.150), channel_id=1, replica_groups=mesh['batch'=16,'tok'=8,'grp'=2] {'tok','grp'}, use_global_device_ids=true, to_apply=%region_18.19 | all-reduce | flops 128 | bytes 1024 | tf_op jit(solution)/shard_map/psum | solution.py:144
  348.2 3.7 fusion.18
  352.0 1.9 copy.207
  354.8 2.0 collective-permute-start.6
  366.6 1.9 fusion.24
  368.5 3.5 fusion.25
  379.0 39.3 %all-reduce.6.cloned.1.call-done = bf16[2432,64]{1,0:T(8,128)(2,1)} async-done(((bf16[2432,64]{1,0:T(8,128)(2,1)}), bf16[2432,64]{1,0:T(8,128)(2,1)}) %all-reduce.6.cloned.1.call-update) | async-done | bytes 311312 | tf_op jit(solution)/shard_map/psum | solution.py:165
  418.3 829.6 %all-reduce.7 = f32[2432,64]{1,0:T(8,128)S(1)} all-reduce(bf16[2432,64]{1,0:T(8,128)(2,1)} %all-reduce.6.cloned.1.call-done), channel_id=2, replica_groups=mesh['batch'=16,'tok'=8,'grp'=2] {'batch','tok'}, use_global_device_ids=true, to_apply=%region_22.23.clone | all-reduce | flops 155648 | bytes 933888
  (225 shorter events, 103.5 us)
Async XLA Ops:
  7.2 207.6 %copy-start = (bf16[512,1024]{1,0:T(8,128)(2,1)S(1)}, bf16[512,1024]{1,0:T(8,128)(2,1)}, u32[]{:S(2)}) copy-start(bf16[512,1024]{1,0:T(8,128)(2,1)} %param.29) | copy-start | bytes 3145732
  7.2 4.7 copy-start.2
  7.2 3.6 copy-start.35
  7.2 4.1 copy-start.18
  7.2 411.1 %all-reduce.6.cloned.1.call-start = ((), (), s32[]{:S(2)}) async-start(), calls=%async_computation | async-start | bytes 1245184 | tf_op jit(solution)/shard_map/psum | solution.py:165
  7.3 4.6 copy-start.17
  7.3 5.3 copy-start.10
  11.9 12.1 copy-start.36
  20.4 15.3 %collective-permute-start = (bf16[2,1,2048]{2,1,0:T(2,128)(2,1)}, bf16[2,1,2048]{2,1,0:T(2,128)(2,1)}, u32[]{:S(2)}, u32[]{:S(2)}) collective-permute-start(bf16[2,1,2048]{2,1,0:T(2,128)(2,1)} %get-tuple-element.43), channel_id=1, source_target_pairs={{0,1},{1,2},{2,3},{3,4},{4,5},{5,6},{6,7},{7,8},{8,9},{9,10},{10,1... | collective-permute-start | bytes 24584 | tf_op jit(solution)/shard_map/ppermute | solution.py:24
  22.7 12.9 %collective-permute-start.1 = (bf16[2,1,2048]{2,1,0:T(2,128)(2,1)}, bf16[2,1,2048]{2,1,0:T(2,128)(2,1)}, u32[]{:S(2)}, u32[]{:S(2)}) collective-permute-start(bf16[2,1,2048]{2,1,0:T(2,128)(2,1)} %get-tuple-element.44), channel_id=1, source_target_pairs={{1,0},{2,1},{3,2},{4,3},{5,4},{6,5},{7,6},{8,7},{9,8},{10,9},{11,1... | collective-permute-start | bytes 24584 | tf_op jit(solution)/shard_map/ppermute | solution.py:25
  36.5 13.4 %copy-start.21 = (pred[16,17]{0,1:T(8,128)(4,1)S(1)}, pred[16,17]{0,1:T(8,128)(4,1)}, u32[]{:S(2)}) copy-start(pred[16,17]{0,1:T(8,128)(4,1)} %constant.108) | copy-start | bytes 820
  36.5 13.4 %copy-start.34 = (f32[512]{0:T(512)S(1)}, f32[512]{0:T(512)}, u32[]{:S(2)}) copy-start(f32[512]{0:T(512)} %param.23) | copy-start | bytes 6148
  118.8 5.4 copy-start.3
  131.3 10.0 collective-permute-start.2
  138.3 4.3 collective-permute-start.3
  142.6 6.5 slice-start
  144.3 4.8 slice-start.1
  214.8 2.7 copy-start.8
  214.8 2.7 copy-start.23
  218.8 2.7 copy-start.12
  223.0 33.4 %copy-start.13 = (bf16[1,16,17,512]{3,1,2,0:T(8,128)(2,1)S(1)}, bf16[1,16,17,512]{3,1,2,0:T(8,128)(2,1)}, u32[]{:S(2)}) copy-start(bf16[1,16,17,512]{3,1,2,0:T(8,128)(2,1)} %get-tuple-element.40) | copy-start | bytes 835588
  249.8 9.3 copy-start.19
  249.8 10.9 copy-start.31
  253.4 9.5 collective-permute-start.4
  257.8 8.4 collective-permute-start.5
  266.3 7.9 slice-start.2
  269.2 5.0 slice-start.3
  354.8 5.6 collective-permute-start.6
  357.6 4.3 collective-permute-start.7
  368.5 5.1 copy-start.9
  368.5 5.1 copy-start.30
  377.2 871.4 %copy-start.1 = (bf16[512,1024]{1,0:T(8,128)(2,1)S(1)}, bf16[512,1024]{1,0:T(8,128)(2,1)}, u32[]{:S(2)}) copy-start(bf16[512,1024]{1,0:T(8,128)(2,1)} %param.29) | copy-start | bytes 3145732
  (18 other events, 33.9 us)
Sparse Core Ops, SparseCore 0:
  376.4 41.8 all-reduce.5
where the time goes:
time: 1260 us
  blocking collectives  1020 us (81%)
  local copies, waits for them, and re-layouts  93.6 us (7%)
  waiting for transfers between devices  41.4 us (3%)
  other arithmetic  38.3 us (3%)
  matrix products  29.3 us (2%)
  between operations  15.9 us (1%)
  starting transfers between devices  14.4 us (1%)
    unnamed x1, blocking collectives  830 us
    psum x1, blocking collectives, local(): lax.psum((jnp.sum(grouped_grad, axis=(1, 3)), jnp.sum(grouped_grad * grou...  58.2 us
    psum x1, blocking collectives, local(): lax.psum(jnp.sum(act_two, axis=(1, 2)), ('tok', 'grp')) / cells  56.4 us
    psum x1, blocking collectives, local(): lax.psum((jnp.sum(grouped, axis=(1, 3)), jnp.sum(grouped * grouped, axis=...  52.5 us
    psum x1, waiting for transfers between devices, local(): lax.psum(weight_term.astype(jnp.bfloat16), 'grp').astype(jnp.float32)  39.3 us
    all_gather x1, blocking collectives, local(): lax.all_gather(decoded[:, None], ('tok', 'grp'), axis=1, tiled=True)  26 us
  transfers between devices with their start and end apart: 9, of which 2 were waited for; matrix products, arithmetic and copies ran while one was open for 3% of the time, Pallas kernels for 0%

commit v1 on v0

v1 whole, which is shorter than its diff:
```python
import jax
import jax.numpy as jnp
from jax import lax
from jax.experimental import pallas as pl
from jax.experimental.pallas import tpu as pltpu
from jax.sharding import PartitionSpec as P

D = 2432
CH = 512
EMB = 1024
GROUP_N = 131072.0
CELLS = 8192.0
EPS = 1e-6
LSCALE = 1.5305
LSHIFT = 0.0609
REWARD_W = 16.0
BF = jnp.bfloat16
F32 = jnp.float32
MESH = pl.DeviceIdType.MESH

NT = (((1,), (1,)), ((), ()))


def mm(a, b):
    return jnp.dot(a, b, preferred_element_type=F32)


def mm_nt(a, b):
    return lax.dot_general(a, b, NT, preferred_element_type=F32)


def iota(shape, dim):
    return lax.broadcasted_iota(jnp.int32, shape, dim)


def one_hot(cond):
    return jnp.where(cond, 1.0, 0.0).astype(BF)


def noise_level(step, shape):
    fraction = (jnp.full(shape, step, jnp.int32).astype(F32) + 1.0) / 1000.0
    return 3.0 * fraction / (1.0 + 2.0 * fraction)


def group_total(tile):
    lane = iota(tile.shape, 1)
    for step in (1, 2, 4, 8):
        tile = tile + jnp.where(
            (lane & step) != 0, pltpu.roll(tile, step, 1), pltpu.roll(tile, 128 - step, 1)
        )
    return tile


def kernel(
    time_ref, map_ref,
    hidden_h, shift_h, scale_h, outw_h, noisy_h, ink_h, inb_h, gain_h, nbias_h,
    midk_h, midb_h, rgb_h, clip_h, text_h,
    hg_h, wg_ref, rew_out, pix_out,
    hid, shiftv, scalev, outw, noisy, ink, inb, gain, nbias, midk, midb, rgb, clip, text,
    stat_m, stat_i, mod, modt, modp, wrep, ve, nl, latsend, rbuf, lhs, wb,
    first, act, slope, gsec, wgr, gfc, rowbuf,
    p1, p2, p3, rewb, pixg, gvsend, gvr, wt, s1send, s1recv, s2send, s2recv, hgv, own_tokens,
    load_sem, lat_s, lat_r, ex_s, ex_r, pix_s, pix_r, rew_s, rew_r, mod_s, mod_r,
    gv_s, gv_r, s1_s, s1_r, s2_s, s2_r, out_sem,
):
    bt = lax.axis_index("batch")
    tok = lax.axis_index("tok")
    c = lax.axis_index("grp")
    y, zh = lax.div(tok, 2), lax.rem(tok, 2)
    zl, x = lax.div(bt, 4), lax.rem(bt, 4)
    j = 2 * y + c

    pairs = [
        (outw_h, outw), (scale_h, scalev), (shift_h, shiftv), (hidden_h, hid),
        (noisy_h, noisy), (ink_h, ink), (inb_h, inb), (gain_h, gain), (nbias_h, nbias),
        (midb_h, midb), (rgb_h, rgb), (midk_h, midk), (clip_h, clip), (text_h, text),
    ]
    loads = [
        pltpu.make_async_copy(src, dst, load_sem.at[i]) for i, (src, dst) in enumerate(pairs)
    ]
    for copy in loads:
        copy.start()

    bar = pltpu.get_barrier_semaphore()
    for d in range(1, 16):
        n = lax.rem(tok * 2 + c + d, 16)
        pl.semaphore_signal(
            bar, inc=1, device_id={"tok": lax.div(n, 2), "grp": lax.rem(n, 2)}, device_id_type=MESH
        )
        n = lax.rem(x * 4 + y + d, 16)
        pl.semaphore_signal(
            bar, inc=1,
            device_id={"batch": zl * 4 + lax.div(n, 4), "tok": lax.rem(n, 4) * 2 + zh},
            device_id_type=MESH,
        )
        n = lax.rem((zl * 2 + zh) * 2 + c + d, 16)
        pl.semaphore_signal(
            bar, inc=1,
            device_id={
                "batch": lax.div(n, 4) * 4 + x,
                "tok": y * 2 + lax.rem(lax.div(n, 2), 2),
                "grp": lax.rem(n, 2),
            },
            device_id_type=MESH,
        )

    loads[0].wait()
    k64, j256 = iota((64, 256), 0), iota((64, 256), 1)
    spread = one_hot(((k64 >> 5) == (j256 >> 7)) & ((k64 & 31) == (j256 & 31)))
    wrep[...] = mm(outw[...], spread).astype(BF)

    for copy in loads[1:4]:
        copy.wait()

    def norm_rows(i, carry):
        img, start = lax.div(i, 4), pl.multiple_of(lax.rem(i, 4) * 32, 32)
        flat = pl.multiple_of(i * 32, 32)
        values = hid[img, pl.ds(start, 32), :].astype(F32)
        mean = jnp.sum(values, axis=-1, keepdims=True) / D
        centered = values - mean
        inv = lax.rsqrt(jnp.sum(centered * centered, axis=-1, keepdims=True) / D + EPS)
        stat_m[pl.ds(flat, 32), :] = mean
        stat_i[pl.ds(flat, 32), :] = inv
        gain_row = 1.0 + scalev[pl.ds(img, 1), :]
        mod[pl.ds(flat, 32), :] = (
            centered * inv * gain_row + shiftv[pl.ds(img, 1), :]
        ).astype(BF)
        return carry

    lax.fori_loop(0, 8, norm_rows, 0)
    velocity = mm(mod[...], wrep[...])
    for a in range(2):
        ve[a] = velocity[:, a * 128 : a * 128 + 128]

    loads[4].wait()
    for i in range(2):
        for b in range(16):
            nl[i, :, b, :] = noisy[i, :, b * 128 : (b + 1) * 128]
    lane_chi = iota((64, 128), 1) >> 5
    vel = [jnp.zeros((64, 128), F32)] * 2
    for chi in range(4):
        for a in range(2):
            vel[a] = jnp.where(lane_chi == chi, ve[a, pl.ds(chi, 64, stride=4), :], vel[a])
    for i in range(2):
        sigma = noise_level(time_ref[i], (16, 128))
        for p in range(2):
            for a in range(2):
                r = 2 * p + a
                part = vel[a][(i * 2 + p) * 16 : (i * 2 + p) * 16 + 16, :]
                latsend[i, r * 16 : r * 16 + 16, :] = (
                    (nl[i, r] - sigma * part) / LSCALE + LSHIFT
                ).astype(BF)

    pl.semaphore_wait(bar, 45)

    main_pos = 1 + c
    halo_j = 2 * y + zh + 2 * c - 1
    halo_pos = 3 - 3 * c
    halo_ok = (halo_j >= 0) & (halo_j <= 7)
    self_main = c == zh

    def lat_copies(h):
        here = zh == h
        main = pltpu.make_async_remote_copy(
            src_ref=latsend.at[h], dst_ref=rbuf.at[main_pos],
            send_sem=lat_s.at[2 * h], recv_sem=lat_r.at[main_pos],
            device_id={"tok": y * 2 + h, "grp": zh}, device_id_type=MESH,
        )
        halo = pltpu.make_async_remote_copy(
            src_ref=latsend.at[h], dst_ref=rbuf.at[halo_pos],
            send_sem=lat_s.at[2 * h + 1], recv_sem=lat_r.at[halo_pos],
            device_id={"tok": lax.div(halo_j, 2) * 2 + h, "grp": lax.rem(halo_j, 2)},
            device_id_type=MESH,
        )
        main_ok = jnp.logical_not(here & self_main)
        far_ok = halo_ok & jnp.logical_not(here & jnp.logical_not(self_main))
        return (main, main_ok), (halo, far_ok)

    for h in range(2):
        for copy, ok in lat_copies(h):
            pl.when(ok)(copy.start)
    self_pos = jnp.where(self_main, main_pos, halo_pos)
    rbuf[self_pos] = latsend[zh]

    @pl.when(j == 0)
    def _():
        rbuf[0] = jnp.zeros((64, 128), BF)

    @pl.when(j == 7)
    def _():
        rbuf[3] = jnp.zeros((64, 128), BF)

    for copy in loads[5:11]:
        copy.wait()

    def clear(i, carry):
        wb[pl.ds(pl.multiple_of(i * 16, 16), 16), :] = jnp.zeros((16, 8 * CH), BF)
        return carry

    lax.fori_loop(0, 32, clear, 0)
    for dy in range(3):
        for dx in range(3):
            tap = ink[dy, dx]
            for o in range(8):
                i = o + dx - 1
                row = 384 + 32 * dy if i < 0 else 384 + 32 * dy + 16 if i > 7 else dy * 128 + 16 * i
                wb[row : row + 16, o * CH : (o + 1) * CH] = tap
    rgbt = mm_nt(one_hot(iota((8, 3), 0) == iota((8, 3), 1)), rgb[...]).astype(BF)

    def wait_lat(pos, ok):
        copy = pltpu.make_async_remote_copy(
            src_ref=latsend.at[0], dst_ref=rbuf.at[pos],
            send_sem=lat_s.at[0], recv_sem=lat_r.at[pos],
            device_id={"tok": tok, "grp": 1 - c}, device_id_type=MESH,
        )
        pl.when(ok & (self_pos != pos))(copy.wait_recv)

    wait_lat(0, j > 0)
    wait_lat(1, j >= 0)
    wait_lat(2, j >= 0)
    wait_lat(3, j < 7)

    lat = rbuf[...].reshape(256, 128)
    lat32 = lat.astype(F32)
    blk = iota((256, 128), 0) & 15
    lane = iota((256, 128), 1)
    after = jnp.where((lane < 16) & (blk < 15), pltpu.roll(lat32, 255, 0), 0.0)
    before = jnp.where((lane >= 112) & (blk > 0), pltpu.roll(lat32, 1, 0), 0.0)
    edge = after + before
    side = sum(
        pltpu.roll(edge, 16 + 32 * dy, 1)[16 * dy : 16 * dy + 224] for dy in range(3)
    )
    for dy in range(3):
        lhs[:, dy * 128 : dy * 128 + 128] = lat[16 * dy : 16 * dy + 224]
    lhs[:, 384:512] = side.astype(BF)

    sum_one = jnp.zeros((8, CH), F32)
    sum_two = jnp.zeros((8, CH), F32)
    for o in range(8):
        out = mm(lhs[...], wb[:, o * CH : (o + 1) * CH]) + inb[...]
        first[:, o] = out.reshape(14, 16, CH)
        own = out[48:176].reshape(16, 8, CH)
        sum_one = sum_one + jnp.sum(own, axis=0)
        sum_two = sum_two + jnp.sum(own * own, axis=0)

    def pack(buf, rows):
        for n, row in enumerate(rows):
            row = jnp.sum(row, axis=0, keepdims=True)
            for k in range(4):
                buf[j, n * 4 + k : n * 4 + k + 1, :] = row[:, k * 128 : k * 128 + 128]

    def exchange(phase, buf):
        copies = []
        for d in range(1, 8):
            n = lax.rem(j + d, 8)
            copies.append(
                pltpu.make_async_remote_copy(
                    src_ref=buf.at[j], dst_ref=buf.at[j],
                    send_sem=ex_s.at[phase, d - 1], recv_sem=ex_r.at[phase, d - 1],
                    device_id={"tok": lax.div(n, 2) * 2 + zh, "grp": lax.rem(n, 2)},
                    device_id_type=MESH,
                )
            )
        for copy in copies:
            copy.start()
        return copies

    def collect(buf, copies):
        for copy in copies:
            copy.wait_recv()
        total = buf[0]
        for k in range(1, 8):
            total = total + buf[k]
        return total

    def as_row(tile, start):
        rowbuf[...] = tile
        return jnp.concatenate([rowbuf[start + k : start + k + 1, :] for k in range(4)], axis=1)

    pack(p1, (sum_one, sum_two))
    ex1 = exchange(0, p1)

    def flip(k, carry):
        start = pl.multiple_of(k * 128, 128)
        modt[pl.ds(start, 128), :] = mod[:, pl.ds(start, 128)].astype(F32).T.astype(BF)
        return carry

    lax.fori_loop(0, 19, flip, 0)
    half = D // 2
    other_start = pl.multiple_of((1 - c) * half, 64)
    mod_copy = pltpu.make_async_remote_copy(
        src_ref=modt.at[pl.ds(other_start, half), :], dst_ref=modp,
        send_sem=mod_s, recv_sem=mod_r,
        device_id={"grp": 1 - c}, device_id_type=MESH,
    )
    mod_copy.start()

    stats = group_total(collect(p1, ex1)) / GROUP_N
    mu = as_row(stats, 0)
    rstd = lax.rsqrt(as_row(stats, 4) - mu * mu + EPS)
    coef_a = rstd * gain[...] * 0.5
    coef_b = (nbias[...] - mu * rstd * gain[...]) * 0.5

    blk16 = iota((16, CH), 0)

    def put_row(buf, r, value):
        buf[r, 1:9] = value.astype(BF)
        buf[r, 0] = jnp.where(blk16 > 0, pltpu.roll(value[7], 1, 0), 0.0).astype(BF)
        buf[r, 9] = jnp.where(blk16 < 15, pltpu.roll(value[0], 15, 0), 0.0).astype(BF)

    def inside(row):
        return ((row >= 0) & (row < 64)).astype(F32)

    def act_row(r, carry):
        half_u = first[r] * coef_a + coef_b
        value = half_u * (1.0 + jnp.tanh(half_u)) * inside(8 * j - 3 + r)
        put_row(act, r, value)
        return carry

    lax.fori_loop(0, 14, act_row, 0)

    loads[11].wait()

    def decode(pieces):
        total = None
        for dy in range(3):
            for dx in range(3):
                part = [act[pl.ds(r + dy, n), dx : dx + 8].reshape(n * 128, CH) for r, n in pieces]
                part = part[0] if len(part) == 1 else jnp.concatenate(part, axis=0)
                term = mm(part, midk[dy, dx])
                total = term if total is None else total + term
        half_u = (total + midb[...]) * 0.5
        tanh = jnp.tanh(half_u)
        grad = 0.5 * ((1.0 + tanh) + half_u * (1.0 - tanh * tanh))
        return half_u * (1.0 + tanh), grad

    def own_decode(i, total):
        r = 2 + 4 * i
        value, grad = decode([(r, 4)])
        slope[pl.ds(r, 4)] = grad.reshape(4, 8, 16, CH)
        pixel = mm_nt(rgbt, value.astype(BF))
        for colour in range(3):
            for row in range(4):
                pixg[zh, j, pl.ds(colour * 8 + 4 * i + row, 1), :] = (
                    pixel[colour : colour + 1, row * 128 : row * 128 + 128]
                )
        return total + jnp.sum(value.reshape(64, 8, CH), axis=0)

    pooled_sum = lax.fori_loop(0, 2, own_decode, jnp.zeros((8, CH), F32))
    pack(p2, (pooled_sum,))
    ex2 = exchange(1, p2)

    pix_copies = []
    for d in range(1, 16):
        n = lax.rem(tok * 2 + c + d, 16)
        pix_copies.append(
            pltpu.make_async_remote_copy(
                src_ref=pixg.at[zh, j], dst_ref=pixg.at[zh, j],
                send_sem=pix_s.at[d - 1], recv_sem=pix_r.at[d - 1],
                device_id={"tok": lax.div(n, 2), "grp": lax.rem(n, 2)}, device_id_type=MESH,
            )
        )
    for copy in pix_copies:
        copy.start()

    _, grad = decode([(0, 2), (10, 2)])
    slope[0:2] = grad[:256].reshape(2, 8, 16, CH)
    slope[10:12] = grad[256:].reshape(2, 8, 16, CH)

    loads[12].wait()
    loads[13].wait()
    pooled = (as_row(collect(p2, ex2), 0) / CELLS).astype(BF)
    feature = mm(jnp.broadcast_to(pooled, (8, CH)), clip[...])
    target = text[pl.ds(zh, 1), :]
    norm_f = jnp.sqrt(jnp.sum(feature * feature, axis=-1, keepdims=True) + EPS)
    norm_t = jnp.sqrt(jnp.sum(target * target, axis=-1, keepdims=True) + EPS)
    reward = jnp.sum(feature * target, axis=-1, keepdims=True) / (norm_f * norm_t)
    grad_feature = (
        REWARD_W * (target / (norm_f * norm_t) - reward * feature / (norm_f * norm_f))
    ).astype(BF)
    grad_act = mm_nt(grad_feature, clip[...])[0:1, :]
    rewb[zh] = jnp.broadcast_to(reward, (8, 128))
    rew_copy = pltpu.make_async_remote_copy(
        src_ref=rewb.at[zh], dst_ref=rewb.at[zh], send_sem=rew_s, recv_sem=rew_r,
        device_id={"tok": y * 2 + 1 - zh}, device_id_type=MESH,
    )
    rew_copy.start()

    def grad_row(r, carry):
        put_row(gsec, r, slope[r] * grad_act * inside(8 * j - 2 + r))
        return carry

    lax.fori_loop(0, 12, grad_row, 0)

    xh_b = mu * rstd

    def back(pieces):
        total = None
        for dy in range(3):
            for dx in range(3):
                part = [
                    gsec[pl.ds(r + 2 - dy, n), 2 - dx : 10 - dx].reshape(n * 128, CH)
                    for r, n in pieces
                ]
                part = part[0] if len(part) == 1 else jnp.concatenate(part, axis=0)
                term = mm_nt(part, midk[dy, dx])
                total = term if total is None else total + term
        value = [first[pl.ds(r + 2, n)].reshape(n * 128, CH) for r, n in pieces]
        value = value[0] if len(value) == 1 else jnp.concatenate(value, axis=0)
        half_u = value * coef_a + coef_b
        tanh = jnp.tanh(half_u)
        grad = 0.5 * ((1.0 + tanh) + half_u * (1.0 - tanh * tanh))
        return total * (grad * gain[...]), value * rstd - xh_b

    def own_back(i, carry):
        r = 1 + 4 * i
        w, xhat = back([(r, 4)])
        wgr[pl.ds(r, 4)] = w.reshape(4, 8, 16, CH)
        return (
            carry[0] + jnp.sum(w.reshape(64, 8, CH), axis=0),
            carry[1] + jnp.sum((w * xhat).reshape(64, 8, CH), axis=0),
        )

    zero = jnp.zeros((8, CH), F32)
    sums = lax.fori_loop(0, 2, own_back, (zero, zero))
    pack(p3, sums)
    ex3 = exchange(2, p3)
    w, _ = back([(0, 1), (9, 1)])
    wgr[0:1] = w[:128].reshape(1, 8, 16, CH)
    wgr[9:10] = w[128:].reshape(1, 8, 16, CH)

    stats = group_total(collect(p3, ex3)) / GROUP_N
    mean_w = as_row(stats, 0)
    mean_x = as_row(stats, 4)
    coef_f = -rstd * rstd * mean_x
    coef_0 = (xh_b * mean_x - mean_w) * rstd

    def first_row(r, carry):
        value = wgr[r] * rstd + first[r + 2] * coef_f + coef_0
        value = (value * inside(8 * j - 1 + r)).astype(BF)
        start = pl.multiple_of(r * 16, 16)
        for o in range(8):
            gfc[pl.ds(start, 16), o * CH : (o + 1) * CH] = value[o]
        return carry

    lax.fori_loop(0, 10, first_row, 0)
    back_y = mm_nt(gfc[...], wb[...])
    grad_lat = jnp.zeros((128, 128), F32)
    edge = jnp.zeros((128, 128), F32)
    lane = iota((128, 128), 1)
    blk = iota((128, 128), 0) & 15
    for dy in range(3):
        start = (2 - dy) * 16
        grad_lat = grad_lat + back_y[start : start + 128, dy * 128 : dy * 128 + 128]
        part = back_y[start : start + 128, 384:512]
        part = jnp.where((lane >> 5) == dy, part, 0.0)
        edge = edge + pltpu.roll(part, (112 - 32 * dy) % 128, 1)
    grad_lat = grad_lat + jnp.where((lane >= 112) & (blk < 15), pltpu.roll(edge, 127, 0), 0.0)
    grad_lat = grad_lat + jnp.where((lane < 16) & (blk > 0), pltpu.roll(edge, 1, 0), 0.0)
    sigma = noise_level(time_ref[zh], (128, 128))
    gvsend[...] = (-sigma * (grad_lat / LSCALE)).astype(BF).reshape(2, 64, 128)

    def gv_copy(e):
        copy = pltpu.make_async_remote_copy(
            src_ref=gvsend, dst_ref=gvr.at[zh],
            send_sem=gv_s.at[e], recv_sem=gv_r.at[zh],
            device_id={"tok": y * 2 + c, "grp": e}, device_id_type=MESH,
        )
        return copy, jnp.logical_not((c == zh) & (c == e))

    for e in range(2):
        copy, ok = gv_copy(e)
        pl.when(ok)(copy.start)

    @pl.when(c == zh)
    def _():
        gvr[zh] = gvsend[...]

    for h in range(2):
        copy = pltpu.make_async_remote_copy(
            src_ref=gvsend, dst_ref=gvr.at[h],
            send_sem=gv_s.at[0], recv_sem=gv_r.at[h],
            device_id={"tok": y * 2 + c, "grp": 0}, device_id_type=MESH,
        )
        pl.when(jnp.logical_not((c == zh) & (zh == h)))(copy.wait_recv)

    def tokens(e):
        for a in range(2):
            rows = [
                gvr[i, e, (2 * p + a) * 16 : (2 * p + a) * 16 + 16, :]
                for i in range(2) for p in range(2)
            ]
            full = jnp.concatenate(rows, axis=0).astype(F32)
            for chi in range(4):
                ve[a, pl.ds(chi, 64, stride=4), :] = jnp.where(lane_chi == chi, full, 0.0)
        return jnp.concatenate([ve[0], ve[1]], axis=1).astype(BF)

    j_r, k_c = iota((256, 256), 0), iota((256, 256), 1)
    target_lane = j_r & 63
    keep = ((target_lane >> 5) == (k_c >> 7)) & ((target_lane & 31) == (k_c & 31))
    quad = one_hot(keep & ((j_r < 64) | (j_r >= 192)))
    mine = tokens(c)
    mine_gv = mm_nt(mine, quad).astype(BF)
    theirs_gv = mm_nt(tokens(1 - c), quad).astype(BF)
    mod_copy.wait_recv()
    own_start = c * half
    term = mm(modt[pl.ds(pl.multiple_of(own_start, 64), 608), :], mine_gv[:, :128])
    term = term + mm(modt[pl.ds(pl.multiple_of(own_start + 608, 32), 608), :], mine_gv[:, 128:])
    term = term + mm(modp[0:608, :], theirs_gv[:, :128])
    term = term + mm(modp[608:1216, :], theirs_gv[:, 128:])
    wt[...] = term * (1.0 / 2048.0)
    for k in range(16):
        s1send[k, 0:32, :] = wt[38 * k : 38 * k + 32, :].astype(BF)
        tail = jnp.concatenate([wt[38 * k + 32 : 38 * k + 38, :], jnp.zeros((10, 128), F32)], axis=0)
        s1send[k, 32:48, :] = tail.astype(BF)
    me_xy = x * 4 + y
    s1 = []
    for d in range(1, 16):
        n = lax.rem(me_xy + d, 16)
        s1.append(
            pltpu.make_async_remote_copy(
                src_ref=s1send.at[n], dst_ref=s1recv.at[me_xy],
                send_sem=s1_s.at[d - 1], recv_sem=s1_r.at[d - 1],
                device_id={"batch": zl * 4 + lax.div(n, 4), "tok": lax.rem(n, 4) * 2 + zh},
                device_id_type=MESH,
            )
        )
    for copy in s1:
        copy.start()
    s1recv[me_xy] = s1send[me_xy]

    own_tokens[...] = mine

    def hidden_rows(i, carry):
        img, start = lax.div(i, 4), pl.multiple_of(lax.rem(i, 4) * 32, 32)
        flat = pl.multiple_of(i * 32, 32)
        grad_mod = mm_nt(own_tokens[pl.ds(flat, 32), :], wrep[...])
        inv = stat_i[pl.ds(flat, 32), :]
        normal = (hid[img, pl.ds(start, 32), :].astype(F32) - stat_m[pl.ds(flat, 32), :]) * inv
        e = grad_mod * (1.0 + scalev[pl.ds(img, 1), :])
        mean_e = jnp.sum(e, axis=-1, keepdims=True) / D
        mean_n = jnp.sum(e * normal, axis=-1, keepdims=True) / D
        hgv[img, pl.ds(start, 32), :] = (inv * (e - mean_e - normal * mean_n)).astype(BF)
        return carry

    lax.fori_loop(0, 8, hidden_rows, 0)
    hg_copy = pltpu.make_async_copy(hgv, hg_h, out_sem)
    hg_copy.start()

    for copy in s1:
        copy.wait_recv()
    total = s1recv[0].astype(F32)
    for k in range(1, 16):
        total = total + s1recv[k].astype(F32)
    wt[0:48, :] = total
    for z in range(2):
        s2send[z] = wt[19 * z : 19 * z + 24, :]
    me_z = zl * 2 + zh

    def line_copy(n):
        dest_zl, dest_zh, dest_c = 2 * c + n // 4, (n // 2) % 2, n % 2
        copy = pltpu.make_async_remote_copy(
            src_ref=s2send.at[dest_zh], dst_ref=s2recv.at[me_z],
            send_sem=s2_s.at[n], recv_sem=s2_r.at[me_z],
            device_id={"batch": dest_zl * 4 + x, "tok": y * 2 + dest_zh, "grp": dest_c},
            device_id_type=MESH,
        )
        return copy, jnp.logical_not((dest_zl == zl) & (dest_zh == zh) & (dest_c == c))

    for n in range(8):
        copy, ok = line_copy(n)
        pl.when(ok)(copy.start)
    self_line = lax.div(zl, 2) == c

    @pl.when(self_line)
    def _():
        s2recv[me_z] = s2send[zh]

    for copy in pix_copies:
        copy.wait_recv()
    l384, k384 = iota((384, 384), 0), iota((384, 384), 1)
    cell = l384 & 127
    place = jnp.where(k384 == ((cell & 15) * 8 + (cell >> 4)) * 3 + (l384 >> 7), 1.0, 0.0)
    for i in range(2):
        slab = map_ref[i, 0]
        block = pixg[i, slab >> 1]
        odd = jnp.full((24, 128), slab & 1, jnp.int32) == 1
        block = jnp.where(odd, pltpu.roll(block, 20, 0), block)
        wide = jnp.concatenate([block[0:8], block[8:16], block[16:24]], axis=1)
        moved = lax.dot_general(
            wide, place, (((1,), (0,)), ((), ())),
            precision=lax.Precision.HIGHEST, preferred_element_type=F32,
        )
        pix_out[i, 0] = moved[0:4]

    rew_copy.wait_recv()
    lane = iota((1, 128), 1)
    rew_out[...] = jnp.where(lane == 0, rewb[0, 0:1, :], rewb[1, 0:1, :])[:, 0:2]

    for n in range(8):
        copy = pltpu.make_async_remote_copy(
            src_ref=s2send.at[0], dst_ref=s2recv.at[n],
            send_sem=s2_s.at[0], recv_sem=s2_r.at[n],
            device_id={"grp": 1 - c}, device_id_type=MESH,
        )
        pl.when(jnp.logical_not(self_line & (me_z == n)))(copy.wait_recv)
    total = s2recv[0]
    for k in range(1, 8):
        total = total + s2recv[k]
    odd = jnp.full((24, 128), lax.rem(zl, 2), jnp.int32) == 1
    total = jnp.where(odd, pltpu.roll(total, 64, 1), total)
    wg_ref[...] = total[0:19, 0:64]

    for h in range(2):
        for copy, ok in lat_copies(h):
            pl.when(ok)(copy.wait_send)
    for copy in ex1 + ex2 + ex3 + pix_copies + s1 + [rew_copy, mod_copy]:
        copy.wait_send()
    for e in range(2):
        copy, ok = gv_copy(e)
        pl.when(ok)(copy.wait_send)
    for n in range(8):
        copy, ok = line_copy(n)
        pl.when(ok)(copy.wait_send)
    hg_copy.wait()


def local(
    hidden, shift, scale, out_weight, noisy_latent, timestep, in_kernel, in_bias,
    norm_gain, norm_bias, mid_kernel, mid_bias, rgb_weight, clip_weight, text_embed, slab_map,
):
    any_spec = pl.BlockSpec(memory_space=pl.ANY)
    smem = pl.BlockSpec(memory_space=pltpu.SMEM)
    vmem = pl.BlockSpec(memory_space=pltpu.VMEM)
    dma = pltpu.SemaphoreType.DMA

    def v(dtype, *shape):
        return pltpu.VMEM(shape, dtype)

    hg, wg, reward, pixels = pl.pallas_call(
        kernel,
        out_shape=(
            jax.ShapeDtypeStruct((2, 128, D), BF),
            jax.ShapeDtypeStruct((19, 64), F32),
            jax.ShapeDtypeStruct((1, 2), F32),
            jax.ShapeDtypeStruct((2, 1, 4, 384), F32),
        ),
        in_specs=[smem, smem] + [any_spec] * 14,
        out_specs=(any_spec, vmem, vmem, vmem),
        scratch_shapes=[
            v(BF, 2, 128, D), v(F32, 2, D), v(F32, 2, D), v(BF, D, 64), v(F32, 2, 4, 2048),
            v(BF, 3, 3, 16, CH), v(F32, 1, CH), v(F32, 1, CH), v(F32, 1, CH),
            v(BF, 3, 3, CH, CH), v(F32, 1, CH), v(BF, CH, 3), v(BF, CH, EMB), v(F32, 2, EMB),
            v(F32, 256, 1), v(F32, 256, 1), v(BF, 256, D), v(BF, D, 256), v(BF, D // 2, 256),
            v(BF, D, 256), v(F32, 2, 256, 128), v(F32, 2, 4, 16, 128), v(BF, 2, 64, 128),
            v(BF, 4, 64, 128), v(BF, 224, 512), v(BF, 512, 8 * CH),
            v(F32, 14, 8, 16, CH), v(BF, 14, 10, 16, CH), v(F32, 12, 8, 16, CH),
            v(BF, 12, 10, 16, CH), v(F32, 10, 8, 16, CH), v(BF, 160, 8 * CH), v(F32, 8, 128),
            v(F32, 8, 8, 128), v(F32, 8, 8, 128), v(F32, 8, 8, 128), v(F32, 2, 8, 128),
            v(F32, 2, 8, 24, 128), v(BF, 2, 64, 128), v(BF, 2, 2, 64, 128), v(F32, 608, 128),
            v(BF, 16, 48, 128), v(BF, 16, 48, 128), v(F32, 2, 24, 128), v(F32, 8, 24, 128),
            v(BF, 2, 128, D), v(BF, 256, 256),
            dma((14,)), dma((4,)), dma((4,)), dma((3, 7)), dma((3, 7)), dma((15,)), dma((15,)),
            dma, dma, dma, dma, dma((2,)), dma((2,)), dma((15,)), dma((15,)), dma((8,)), dma((8,)),
            dma,
        ],
        compiler_params=pltpu.CompilerParams(
            collective_id=0, has_side_effects=True, vmem_limit_bytes=58 * 2**20
        ),
    )(
        timestep, slab_map, hidden, shift, scale, out_weight, noisy_latent, in_kernel,
        in_bias.reshape(1, CH), norm_gain.reshape(1, CH), norm_bias.reshape(1, CH),
        mid_kernel, mid_bias.reshape(1, CH), rgb_weight, clip_weight, text_embed,
    )
    return hg, wg, reward.reshape(2), pixels


def solution(mesh):
    rows = ("tok", "grp")
    return jax.shard_map(
        local,
        mesh=mesh,
        in_specs=(
            P("batch", rows, None), P("batch", None), P("batch", None), P(),
            P("batch", rows, None), P("batch"), P(), P(), P(), P(), P(), P(), P(), P(),
            P("batch", None), P("batch", rows),
        ),
        out_specs=(
            P("batch", rows, None), P(("batch", "tok"), None), P("batch"),
            P("batch", rows, None, None),
        ),
        check_vma=False,
    )
```

time: 1260 us -> 74.8 us (0.06)
  the two profiles are of different devices: /device:TPU:64 before, /device:TPU:1 now
where the time goes in v1:
time: 74.8 us; the launch traced here: 74.6 us
  Pallas kernels  64.9 us (87%)
  local copies, waits for them, and re-layouts  8.96 us (12%)
    pallas_call x1, Pallas kernels, local(): pl.pallas_call(kernel, out_shape=(jax.ShapeDtypeStruct((2, 128, D), BF),...  64.9 us
    unnamed x13, local copies, waits for them, and re-layouts  8.96 us

profile of v1, /device:TPU:1, one launch (start us, length us, event | category | flops | bytes accessed | tf_op | source)
XLA Modules:
  0.0 74.6 jit_solution(9125777835214701034)
XLA Ops:
  0.6 1.3 %copy.20.map_ref = s32[2,1]{1,0:T(2,128)} copy(s32[2,1]{0,1:T(1,128)} %param.31) | data formatting | bytes 16 | tf_op args[15]
  1.9 1.5 %copy.22.rgb_h = bf16[512,3]{1,0:T(8,128)(2,1)} copy(bf16[512,3]{0,1:T(4,128)(2,1)} %param.28) | data formatting | bytes 6144 | tf_op args[12]
  3.4 2.0 %copy.21.outw_h = bf16[2432,64]{1,0:T(8,128)(2,1)} copy(bf16[2432,64]{0,1:T(8,128)(2,1)} %param.19) | data formatting | bytes 622592 | tf_op args[3]
  5.4 64.9 %shard_map.183 = (bf16[2,128,2432]{2,1,0:T(8,128)(2,1)}, f32[19,64]{1,0:T(8,128)}, f32[1,2]{1,0:T(1,128)}, f32[2,1,4,384]{3,2,1,0:T(4,128)}) custom-call(s32[2]{0:T(128)} %time_ref.1, s32[2,1]{1,0:T(2,128)} %copy.20.map_ref, bf16[2,128,2432]{2,1,0:T(8,128)(2,1)} %hidden_h.1, f32[2,2432]{1,0:T(2,128)} %shift_h.1, f32[2,2432]{1,0:T(2,128)} %scale_h.1, ...), custom_call_target="tpu_custom_call" | custom-call | tf_op jit(solution)/shard_map/pallas_call | solution.py:640
  70.4 0.0 copy-start.1
  70.4 0.0 copy-start.2
  70.4 0.0 copy-start
  70.4 2.4 %copy.27 = bf16[2,128,2432]{2,1,0:T(8,128)(2,1)} copy(bf16[2,128,2432]{2,1,0:T(8,128)(2,1)} %get-tuple-element.16) | data formatting | bytes 2490368
  72.9 0.0 copy-done.1
  72.9 0.6 copy.28
  73.5 0.0 copy-done.2
  73.5 0.5 copy.29
  74.0 0.0 copy-done
  74.0 0.6 copy.30
Async XLA Ops:
  70.4 2.5 %copy-start.1 = (f32[19,64]{1,0:T(8,128)S(1)}, f32[19,64]{1,0:T(8,128)}, u32[]{:S(2)}) copy-start(f32[19,64]{1,0:T(8,128)} %get-tuple-element.17) | copy-start | bytes 14596
  70.4 3.0 %copy-start.2 = (f32[1,2]{1,0:T(1,128)S(1)}, f32[1,2]{1,0:T(1,128)}, u32[]{:S(2)}) copy-start(f32[1,2]{1,0:T(1,128)} %get-tuple-element.10) | copy-start | bytes 28
  70.4 3.6 %copy-start = (f32[2,1,4,384]{3,2,1,0:T(4,128)S(1)}, f32[2,1,4,384]{3,2,1,0:T(4,128)}, u32[]{:S(2)}) copy-start(f32[2,1,4,384]{3,2,1,0:T(4,128)} %get-tuple-element.19) | copy-start | bytes 36868

commit v2 on v1

--- a/solution.py
+++ b/solution.py
@@ -55,13 +55,13 @@
     time_ref, map_ref,
     hidden_h, shift_h, scale_h, outw_h, noisy_h, ink_h, inb_h, gain_h, nbias_h,
     midk_h, midb_h, rgb_h, clip_h, text_h,
-    hg_h, wg_ref, rew_out, pix_out,
+    hgv, wg_ref, rew_out, pix_out,
     hid, shiftv, scalev, outw, noisy, ink, inb, gain, nbias, midk, midb, rgb, clip, text,
     stat_m, stat_i, mod, modt, modp, wrep, ve, nl, latsend, rbuf, lhs, wb,
     first, act, slope, gsec, wgr, gfc, rowbuf,
-    p1, p2, p3, rewb, pixg, gvsend, gvr, wt, s1send, s1recv, s2send, s2recv, hgv, own_tokens,
+    p1, p2, p3, rewb, pixg, gvx, gvr, wt, s1send, s1recv, s2send, s2recv, own_tokens,
     load_sem, lat_s, lat_r, ex_s, ex_r, pix_s, pix_r, rew_s, rew_r, mod_s, mod_r,
-    gv_s, gv_r, s1_s, s1_r, s2_s, s2_r, out_sem,
+    gx_s, gx_r, gv_s, gv_r, s1_s, s1_r, s2_s, s2_r,
 ):
     bt = lax.axis_index("batch")
     tok = lax.axis_index("tok")
@@ -105,9 +105,9 @@
         )
 
     loads[0].wait()
-    k64, j256 = iota((64, 256), 0), iota((64, 256), 1)
+    j256, k64 = iota((256, 64), 0), iota((256, 64), 1)
     spread = one_hot(((k64 >> 5) == (j256 >> 7)) & ((k64 & 31) == (j256 & 31)))
-    wrep[...] = mm(outw[...], spread).astype(BF)
+    wrep[...] = mm(spread, outw[...]).astype(BF)
 
     for copy in loads[1:4]:
         copy.wait()
@@ -128,7 +128,7 @@
         return carry
 
     lax.fori_loop(0, 8, norm_rows, 0)
-    velocity = mm(mod[...], wrep[...])
+    velocity = mm_nt(mod[...], wrep[...])
     for a in range(2):
         ve[a] = velocity[:, a * 128 : a * 128 + 128]
 
@@ -205,7 +205,7 @@
                 i = o + dx - 1
                 row = 384 + 32 * dy if i < 0 else 384 + 32 * dy + 16 if i > 7 else dy * 128 + 16 * i
                 wb[row : row + 16, o * CH : (o + 1) * CH] = tap
-    rgbt = mm_nt(one_hot(iota((8, 3), 0) == iota((8, 3), 1)), rgb[...]).astype(BF)
+    rgbt = mm(one_hot(iota((8, 3), 0) == iota((8, 3), 1)), rgb[...]).astype(BF)
 
     def wait_lat(pos, ok):
         copy = pltpu.make_async_remote_copy(
@@ -282,18 +282,30 @@
 
     def flip(k, carry):
         start = pl.multiple_of(k * 128, 128)
-        modt[pl.ds(start, 128), :] = mod[:, pl.ds(start, 128)].astype(F32).T.astype(BF)
+        for h in range(2):
+            block = mod[h * 128 : h * 128 + 128, pl.ds(start, 128)]
+            modt[h, pl.ds(start, 128), :] = block.astype(F32).T.astype(BF)
         return carry
 
     lax.fori_loop(0, 19, flip, 0)
     half = D // 2
-    other_start = pl.multiple_of((1 - c) * half, 64)
-    mod_copy = pltpu.make_async_remote_copy(
-        src_ref=modt.at[pl.ds(other_start, half), :], dst_ref=modp,
-        send_sem=mod_s, recv_sem=mod_r,
-        device_id={"grp": 1 - c}, device_id_type=MESH,
-    )
-    mod_copy.start()
+    place4 = zh * 2 + c
+    mod_lane = pl.ds(pl.multiple_of(place4 * 128, 128), 128)
+    mod_copies = []
+    for d in range(1, 4):
+        n = lax.rem(place4 + d, 4)
+        h, core = lax.div(n, 2), lax.rem(n, 2)
+        mod_copies.append(
+            pltpu.make_async_remote_copy(
+                src_ref=modt.at[h, pl.ds(pl.multiple_of(core * half, 64), half), :],
+                dst_ref=modp.at[:, mod_lane],
+                send_sem=mod_s.at[d - 1], recv_sem=mod_r.at[d - 1],
+                device_id={"tok": y * 2 + h, "grp": core}, device_id_type=MESH,
+            )
+        )
+    for copy in mod_copies:
+        copy.start()
+    modp[:, mod_lane] = modt[zh, pl.ds(pl.multiple_of(c * half, 64), half), :]
 
     stats = group_total(collect(p1, ex1)) / GROUP_N
     mu = as_row(stats, 0)
@@ -325,7 +337,7 @@
         total = None
         for dy in range(3):
             for dx in range(3):
-                part = [act[pl.ds(r + dy, n), dx : dx + 8].reshape(n * 128, CH) for r, n in pieces]
+                part = [act[r + dy : r + dy + n, dx : dx + 8].reshape(n * 128, CH) for r, n in pieces]
                 part = part[0] if len(part) == 1 else jnp.concatenate(part, axis=0)
                 term = mm(part, midk[dy, dx])
                 total = term if total is None else total + term
@@ -334,19 +346,18 @@
         grad = 0.5 * ((1.0 + tanh) + half_u * (1.0 - tanh * tanh))
         return half_u * (1.0 + tanh), grad
 
-    def own_decode(i, total):
-        r = 2 + 4 * i
-        value, grad = decode([(r, 4)])
-        slope[pl.ds(r, 4)] = grad.reshape(4, 8, 16, CH)
+    pooled_sum = jnp.zeros((8, CH), F32)
+    for i in range(4):
+        r = 2 + 2 * i
+        value, grad = decode([(r, 2)])
+        slope[r : r + 2] = grad.reshape(2, 8, 16, CH)
         pixel = mm_nt(rgbt, value.astype(BF))
         for colour in range(3):
-            for row in range(4):
-                pixg[zh, j, pl.ds(colour * 8 + 4 * i + row, 1), :] = (
-                    pixel[colour : colour + 1, row * 128 : row * 128 + 128]
-                )
-        return total + jnp.sum(value.reshape(64, 8, CH), axis=0)
-
-    pooled_sum = lax.fori_loop(0, 2, own_decode, jnp.zeros((8, CH), F32))
+            for row in range(2):
+                at = colour * 8 + 2 * i + row
+                pixg[zh, j, at : at + 1, :] = pixel[colour : colour + 1, row * 128 : row * 128 + 128]
+        pooled_sum = pooled_sum + jnp.sum(value.reshape(32, 8, CH), axis=0)
+
     pack(p2, (pooled_sum,))
     ex2 = exchange(1, p2)
 
@@ -399,30 +410,26 @@
         for dy in range(3):
             for dx in range(3):
                 part = [
-                    gsec[pl.ds(r + 2 - dy, n), 2 - dx : 10 - dx].reshape(n * 128, CH)
+                    gsec[r + 2 - dy : r + 2 - dy + n, 2 - dx : 10 - dx].reshape(n * 128, CH)
                     for r, n in pieces
                 ]
                 part = part[0] if len(part) == 1 else jnp.concatenate(part, axis=0)
                 term = mm_nt(part, midk[dy, dx])
                 total = term if total is None else total + term
-        value = [first[pl.ds(r + 2, n)].reshape(n * 128, CH) for r, n in pieces]
+        value = [first[r + 2 : r + 2 + n].reshape(n * 128, CH) for r, n in pieces]
         value = value[0] if len(value) == 1 else jnp.concatenate(value, axis=0)
         half_u = value * coef_a + coef_b
         tanh = jnp.tanh(half_u)
         grad = 0.5 * ((1.0 + tanh) + half_u * (1.0 - tanh * tanh))
         return total * (grad * gain[...]), value * rstd - xh_b
 
-    def own_back(i, carry):
-        r = 1 + 4 * i
-        w, xhat = back([(r, 4)])
-        wgr[pl.ds(r, 4)] = w.reshape(4, 8, 16, CH)
-        return (
-            carry[0] + jnp.sum(w.reshape(64, 8, CH), axis=0),
-            carry[1] + jnp.sum((w * xhat).reshape(64, 8, CH), axis=0),
-        )
-
-    zero = jnp.zeros((8, CH), F32)
-    sums = lax.fori_loop(0, 2, own_back, (zero, zero))
+    sums = [jnp.zeros((8, CH), F32)] * 2
+    for i in range(4):
+        r = 1 + 2 * i
+        w, xhat = back([(r, 2)])
+        wgr[r : r + 2] = w.reshape(2, 8, 16, CH)
+        sums[0] = sums[0] + jnp.sum(w.reshape(32, 8, CH), axis=0)
+        sums[1] = sums[1] + jnp.sum((w * xhat).reshape(32, 8, CH), axis=0)
     pack(p3, sums)
     ex3 = exchange(2, p3)
     w, _ = back([(0, 1), (9, 1)])
@@ -458,11 +465,17 @@
     grad_lat = grad_lat + jnp.where((lane >= 112) & (blk < 15), pltpu.roll(edge, 127, 0), 0.0)
     grad_lat = grad_lat + jnp.where((lane < 16) & (blk > 0), pltpu.roll(edge, 1, 0), 0.0)
     sigma = noise_level(time_ref[zh], (128, 128))
-    gvsend[...] = (-sigma * (grad_lat / LSCALE)).astype(BF).reshape(2, 64, 128)
+    gvx[c] = (-sigma * (grad_lat / LSCALE)).astype(BF).reshape(2, 64, 128)
+
+    gv_pair = pltpu.make_async_remote_copy(
+        src_ref=gvx.at[c], dst_ref=gvx.at[c], send_sem=gx_s, recv_sem=gx_r,
+        device_id={"grp": 1 - c}, device_id_type=MESH,
+    )
+    gv_pair.start()
 
     def gv_copy(e):
         copy = pltpu.make_async_remote_copy(
-            src_ref=gvsend, dst_ref=gvr.at[zh],
+            src_ref=gvx.at[c, e], dst_ref=gvr.at[zh],
             send_sem=gv_s.at[e], recv_sem=gv_r.at[zh],
             device_id={"tok": y * 2 + c, "grp": e}, device_id_type=MESH,
         )
@@ -474,21 +487,12 @@
 
     @pl.when(c == zh)
     def _():
-        gvr[zh] = gvsend[...]
-
-    for h in range(2):
-        copy = pltpu.make_async_remote_copy(
-            src_ref=gvsend, dst_ref=gvr.at[h],
-            send_sem=gv_s.at[0], recv_sem=gv_r.at[h],
-            device_id={"tok": y * 2 + c, "grp": 0}, device_id_type=MESH,
-        )
-        pl.when(jnp.logical_not((c == zh) & (zh == h)))(copy.wait_recv)
-
-    def tokens(e):
+        gvr[zh] = gvx[c, c]
+
+    def tokens(parts):
         for a in range(2):
             rows = [
-                gvr[i, e, (2 * p + a) * 16 : (2 * p + a) * 16 + 16, :]
-                for i in range(2) for p in range(2)
+                part[(2 * p + a) * 16 : (2 * p + a) * 16 + 16, :] for part in parts for p in range(2)
             ]
             full = jnp.concatenate(rows, axis=0).astype(F32)
             for chi in range(4):
@@ -499,16 +503,17 @@
     target_lane = j_r & 63
     keep = ((target_lane >> 5) == (k_c >> 7)) & ((target_lane & 31) == (k_c & 31))
     quad = one_hot(keep & ((j_r < 64) | (j_r >= 192)))
-    mine = tokens(c)
-    mine_gv = mm_nt(mine, quad).astype(BF)
-    theirs_gv = mm_nt(tokens(1 - c), quad).astype(BF)
-    mod_copy.wait_recv()
-    own_start = c * half
-    term = mm(modt[pl.ds(pl.multiple_of(own_start, 64), 608), :], mine_gv[:, :128])
-    term = term + mm(modt[pl.ds(pl.multiple_of(own_start + 608, 32), 608), :], mine_gv[:, 128:])
-    term = term + mm(modp[0:608, :], theirs_gv[:, :128])
-    term = term + mm(modp[608:1216, :], theirs_gv[:, 128:])
-    wt[...] = term * (1.0 / 2048.0)
+    for copy in mod_copies:
+        copy.wait_recv()
+
+    def term_of(row):
+        grads = mm_nt(tokens([gvx[row, 0], gvx[row, 1]]), quad).astype(BF)
+        lanes = pl.ds(pl.multiple_of(row * 256, 256), 256)
+        return mm(modp[0:608, lanes], grads[:, :128]) + mm(modp[608:1216, lanes], grads[:, 128:])
+
+    wt[...] = term_of(c) * (1.0 / 2048.0)
+    gv_pair.wait_recv()
+    wt[...] += term_of(1 - c) * (1.0 / 2048.0)
     for k in range(16):
         s1send[k, 0:32, :] = wt[38 * k : 38 * k + 32, :].astype(BF)
         tail = jnp.concatenate([wt[38 * k + 32 : 38 * k + 38, :], jnp.zeros((10, 128), F32)], axis=0)
@@ -529,12 +534,19 @@
         copy.start()
     s1recv[me_xy] = s1send[me_xy]
 
-    own_tokens[...] = mine
+    for h in range(2):
+        copy = pltpu.make_async_remote_copy(
+            src_ref=gvx.at[0, 0], dst_ref=gvr.at[h],
+            send_sem=gv_s.at[0], recv_sem=gv_r.at[h],
+            device_id={"tok": y * 2 + c, "grp": 0}, device_id_type=MESH,
+        )
+        pl.when(jnp.logical_not((c == zh) & (zh == h)))(copy.wait_recv)
+    own_tokens[...] = tokens([gvr[0], gvr[1]])
 
     def hidden_rows(i, carry):
         img, start = lax.div(i, 4), pl.multiple_of(lax.rem(i, 4) * 32, 32)
         flat = pl.multiple_of(i * 32, 32)
-        grad_mod = mm_nt(own_tokens[pl.ds(flat, 32), :], wrep[...])
+        grad_mod = mm(own_tokens[pl.ds(flat, 32), :], wrep[...])
         inv = stat_i[pl.ds(flat, 32), :]
         normal = (hid[img, pl.ds(start, 32), :].astype(F32) - stat_m[pl.ds(flat, 32), :]) * inv
         e = grad_mod * (1.0 + scalev[pl.ds(img, 1), :])
@@ -544,8 +556,6 @@
         return carry
 
     lax.fori_loop(0, 8, hidden_rows, 0)
-    hg_copy = pltpu.make_async_copy(hgv, hg_h, out_sem)
-    hg_copy.start()
 
     for copy in s1:
         copy.wait_recv()
@@ -582,7 +592,7 @@
     cell = l384 & 127
     place = jnp.where(k384 == ((cell & 15) * 8 + (cell >> 4)) * 3 + (l384 >> 7), 1.0, 0.0)
     for i in range(2):
-        slab = map_ref[i, 0]
+        slab = map_ref[i]
         block = pixg[i, slab >> 1]
         odd = jnp.full((24, 128), slab & 1, jnp.int32) == 1
         block = jnp.where(odd, pltpu.roll(block, 20, 0), block)
@@ -614,7 +624,7 @@
     for h in range(2):
         for copy, ok in lat_copies(h):
             pl.when(ok)(copy.wait_send)
-    for copy in ex1 + ex2 + ex3 + pix_copies + s1 + [rew_copy, mod_copy]:
+    for copy in ex1 + ex2 + ex3 + pix_copies + s1 + mod_copies + [rew_copy, gv_pair]:
         copy.wait_send()
     for e in range(2):
         copy, ok = gv_copy(e)
@@ -622,7 +632,15 @@
     for n in range(8):
         copy, ok = line_copy(n)
         pl.when(ok)(copy.wait_send)
-    hg_copy.wait()
+
+
+def hand_out(*refs):
+    sem = refs[8]
+    copies = [pltpu.make_async_copy(refs[i], refs[4 + i], sem.at[i]) for i in range(4)]
+    for copy in copies:
+        copy.start()
+    for copy in copies:
+        copy.wait()
 
 
 def local(
@@ -640,38 +658,49 @@
     hg, wg, reward, pixels = pl.pallas_call(
         kernel,
         out_shape=(
+            pltpu.VMEM((2, 128, D), BF),
+            pltpu.VMEM((19, 64), F32),
+            pltpu.VMEM((1, 2), F32),
+            pltpu.VMEM((2, 1, 4, 384), F32),
+        ),
+        in_specs=[smem, smem] + [any_spec] * 14,
+        out_specs=(vmem, vmem, vmem, vmem),
+        scratch_shapes=[
+            v(BF, 2, 128, D), v(F32, 2, D), v(F32, 2, D), v(BF, 64, D), v(F32, 2, 4, 2048),
+            v(BF, 3, 3, 16, CH), v(F32, 1, CH), v(F32, 1, CH), v(F32, 1, CH),
+            v(BF, 3, 3, CH, CH), v(F32, 1, CH), v(BF, 3, CH), v(BF, CH, EMB), v(F32, 2, EMB),
+            v(F32, 256, 1), v(F32, 256, 1), v(BF, 256, D), v(BF, 2, D, 128), v(BF, D // 2, 512),
+            v(BF, 256, D), v(F32, 2, 256, 128), v(F32, 2, 4, 16, 128), v(BF, 2, 64, 128),
+            v(BF, 4, 64, 128), v(BF, 224, 512), v(BF, 512, 8 * CH),
+            v(F32, 14, 8, 16, CH), v(BF, 14, 10, 16, CH), v(F32, 12, 8, 16, CH),
+            v(BF, 12, 10, 16, CH), v(F32, 10, 8, 16, CH), v(BF, 160, 8 * CH), v(F32, 8, 128),
+            v(F32, 8, 8, 128), v(F32, 8, 8, 128), v(F32, 8, 8, 128), v(F32, 2, 8, 128),
+            v(F32, 2, 8, 24, 128), v(BF, 2, 2, 64, 128), v(BF, 2, 64, 128), v(F32, 608, 128),
+            v(BF, 16, 48, 128), v(BF, 16, 48, 128), v(F32, 2, 24, 128), v(F32, 8, 24, 128),
+            v(BF, 256, 256),
+            dma((14,)), dma((4,)), dma((4,)), dma((3, 7)), dma((3, 7)), dma((15,)), dma((15,)),
+            dma, dma, dma((3,)), dma((3,)), dma, dma, dma((2,)), dma((2,)), dma((15,)), dma((15,)), dma((8,)), dma((8,)),
+        ],
+        compiler_params=pltpu.CompilerParams(
+            collective_id=0, has_side_effects=True, vmem_limit_bytes=58 * 2**20
+        ),
+    )(
+        timestep, slab_map.reshape(2), hidden, shift, scale, out_weight.T, noisy_latent, in_kernel,
+        in_bias.reshape(1, CH), norm_gain.reshape(1, CH), norm_bias.reshape(1, CH),
+        mid_kernel, mid_bias.reshape(1, CH), rgb_weight.T, clip_weight, text_embed,
+    )
+    hg, wg, reward, pixels = pl.pallas_call(
+        hand_out,
+        out_shape=(
             jax.ShapeDtypeStruct((2, 128, D), BF),
             jax.ShapeDtypeStruct((19, 64), F32),
             jax.ShapeDtypeStruct((1, 2), F32),
             jax.ShapeDtypeStruct((2, 1, 4, 384), F32),
         ),
-        in_specs=[smem, smem] + [any_spec] * 14,
-        out_specs=(any_spec, vmem, vmem, vmem),
-        scratch_shapes=[
-            v(BF, 2, 128, D), v(F32, 2, D), v(F32, 2, D), v(BF, D, 64), v(F32, 2, 4, 2048),
-            v(BF, 3, 3, 16, CH), v(F32, 1, CH), v(F32, 1, CH), v(F32, 1, CH),
-            v(BF, 3, 3, CH, CH), v(F32, 1, CH), v(BF, CH, 3), v(BF, CH, EMB), v(F32, 2, EMB),
-            v(F32, 256, 1), v(F32, 256, 1), v(BF, 256, D), v(BF, D, 256), v(BF, D // 2, 256),
-            v(BF, D, 256), v(F32, 2, 256, 128), v(F32, 2, 4, 16, 128), v(BF, 2, 64, 128),
-            v(BF, 4, 64, 128), v(BF, 224, 512), v(BF, 512, 8 * CH),
-            v(F32, 14, 8, 16, CH), v(BF, 14, 10, 16, CH), v(F32, 12, 8, 16, CH),
-            v(BF, 12, 10, 16, CH), v(F32, 10, 8, 16, CH), v(BF, 160, 8 * CH), v(F32, 8, 128),
-            v(F32, 8, 8, 128), v(F32, 8, 8, 128), v(F32, 8, 8, 128), v(F32, 2, 8, 128),
-            v(F32, 2, 8, 24, 128), v(BF, 2, 64, 128), v(BF, 2, 2, 64, 128), v(F32, 608, 128),
-            v(BF, 16, 48, 128), v(BF, 16, 48, 128), v(F32, 2, 24, 128), v(F32, 8, 24, 128),
-            v(BF, 2, 128, D), v(BF, 256, 256),
-            dma((14,)), dma((4,)), dma((4,)), dma((3, 7)), dma((3, 7)), dma((15,)), dma((15,)),
-            dma, dma, dma, dma, dma((2,)), dma((2,)), dma((15,)), dma((15,)), dma((8,)), dma((8,)),
-            dma,
-        ],
-        compiler_params=pltpu.CompilerParams(
-            collective_id=0, has_side_effects=True, vmem_limit_bytes=58 * 2**20
-        ),
-    )(
-        timestep, slab_map, hidden, shift, scale, out_weight, noisy_latent, in_kernel,
-        in_bias.reshape(1, CH), norm_gain.reshape(1, CH), norm_bias.reshape(1, CH),
-        mid_kernel, mid_bias.reshape(1, CH), rgb_weight, clip_weight, text_embed,
-    )
+        in_specs=[vmem] * 4,
+        out_specs=[any_spec] * 4,
+        scratch_shapes=[dma((4,))],
+    )(hg, wg, reward, pixels)
     return hg, wg, reward.reshape(2), pixels
 
 

time: 74.8 us -> 70.7 us (0.945)
  local copies, waits for them, and re-layouts: 8.96 us -> 2.76 us
  Pallas kernels: 64.9 us -> 67 us
    unnamed x13 -> x8, local copies, waits for them, and re-layouts: 8.96 us -> 2.76 us
    pallas_call x1 -> x2, Pallas kernels: 64.9 us -> 67 us  [the longest x1 64.6 us: local(): pl.pallas_call(kernel, out_shape=(pltpu.VMEM((2, 128, D), BF), pltpu.VMEM...]
where the time goes in v2:
time: 70.7 us; the launch traced here: 70.6 us
  Pallas kernels  67 us (95%)
  local copies, waits for them, and re-layouts  2.76 us (4%)
  between operations  0.82 us (1%)
    pallas_call x1, Pallas kernels, local(): pl.pallas_call(kernel, out_shape=(pltpu.VMEM((2, 128, D), BF), pltpu.VMEM...  64.6 us
    unnamed x8, local copies, waits for them, and re-layouts  2.76 us
    pallas_call x1, Pallas kernels, local(): pl.pallas_call(hand_out, out_shape=(jax.ShapeDtypeStruct((2, 128, D), BF)...  2.39 us

profile of v2, /device:TPU:1, one launch (start us, length us, event | category | flops | bytes accessed | tf_op | source)
XLA Modules:
  0.0 70.6 jit_solution(11902611551324568779)
XLA Ops:
  0.6 64.6 %shard_map.183 = (bf16[2,128,2432]{2,1,0:T(8,128)(2,1)S(1)}, f32[19,64]{1,0:T(8,128)S(1)}, f32[1,2]{1,0:T(1,128)S(1)}, f32[2,1,4,384]{3,2,1,0:T(4,128)S(1)}) custom-call(s32[2]{0:T(128)} %time_ref.1, s32[2]{0:T(128)} %bitcast.14, bf16[2,128,2432]{2,1,0:T(8,128)(2,1)} %hidden_h.1, f32[2,2432]{1,0:T(2,128)} %shift_h.1, f32[2,2432]{1,0:T(2,128)} %scale_h.1, ...), custom_call_target="tpu_custom_call" | custom-call | tf_op jit(solution)/shard_map/pallas_call | solution.py:658
  65.2 0.0 copy-start
  65.3 1.0 %copy-done = bf16[2,128,2432]{2,1,0:T(8,128)(2,1)} copy-done((bf16[2,128,2432]{2,1,0:T(8,128)(2,1)}, bf16[2,128,2432]{2,1,0:T(8,128)(2,1)S(1)}, u32[]{:S(2)}) %copy-start) | copy-done | bytes 1245208
  66.3 0.0 copy-start.1
  66.3 0.6 copy-done.1
  66.9 0.0 copy-start.2
  66.9 0.6 copy-done.2
  67.5 0.0 copy-start.3
  67.5 0.5 copy-done.3
  68.0 2.4 %shard_map.184 = (bf16[2,128,2432]{2,1,0:T(8,128)(2,1)}, f32[19,64]{1,0:T(8,128)}, f32[1,2]{1,0:T(1,128)}, f32[2,1,4,384]{3,2,1,0:T(4,128)}) custom-call(bf16[2,128,2432]{2,1,0:T(8,128)(2,1)} %copy-done, f32[19,64]{1,0:T(8,128)} %copy-done.1, f32[1,2]{1,0:T(1,128)} %copy-done.3, f32[2,1,4,384]{3,2,1,0:T(4,128)} %copy-done.2), custom_call_target="tpu_custom_call" | custom-call | tf_op jit(solution)/shard_map/pallas_call | solution.py:692
Async XLA Ops:
  65.2 1.0 %copy-start = (bf16[2,128,2432]{2,1,0:T(8,128)(2,1)}, bf16[2,128,2432]{2,1,0:T(8,128)(2,1)S(1)}, u32[]{:S(2)}) copy-start(bf16[2,128,2432]{2,1,0:T(8,128)(2,1)S(1)} %get-tuple-element.12.refs_0_) | copy-start | bytes 3735556
  66.3 0.6 copy-start.1
  66.9 0.6 copy-start.2
  67.5 0.5 copy-start.3

commit v3 on v2

--- a/solution.py
+++ b/solution.py
@@ -78,31 +78,25 @@
     loads = [
         pltpu.make_async_copy(src, dst, load_sem.at[i]) for i, (src, dst) in enumerate(pairs)
     ]
-    for copy in loads:
+    for copy in loads[:4]:
         copy.start()
 
     bar = pltpu.get_barrier_semaphore()
-    for d in range(1, 16):
+
+    def greet(**where):
+        pl.semaphore_signal(bar, inc=1, device_id=where, device_id_type=MESH)
+
+    for d in range(15, 0, -1):
         n = lax.rem(tok * 2 + c + d, 16)
-        pl.semaphore_signal(
-            bar, inc=1, device_id={"tok": lax.div(n, 2), "grp": lax.rem(n, 2)}, device_id_type=MESH
-        )
-        n = lax.rem(x * 4 + y + d, 16)
-        pl.semaphore_signal(
-            bar, inc=1,
-            device_id={"batch": zl * 4 + lax.div(n, 4), "tok": lax.rem(n, 4) * 2 + zh},
-            device_id_type=MESH,
-        )
-        n = lax.rem((zl * 2 + zh) * 2 + c + d, 16)
-        pl.semaphore_signal(
-            bar, inc=1,
-            device_id={
-                "batch": lax.div(n, 4) * 4 + x,
-                "tok": y * 2 + lax.rem(lax.div(n, 2), 2),
-                "grp": lax.rem(n, 2),
-            },
-            device_id_type=MESH,
-        )
+        greet(tok=lax.div(n, 2), grp=lax.rem(n, 2))
+    for dz in range(1, 4):
+        for n in range(4):
+            greet(batch=lax.rem(zl + dz, 4) * 4 + x, tok=y * 2 + n // 2, grp=n % 2)
+    for dx in range(1, 4):
+        for dy in range(4):
+            greet(batch=zl * 4 + lax.rem(x + dx, 4), tok=lax.rem(y + dy, 4) * 2 + zh)
+    for copy in loads[4:]:
+        copy.start()
 
     loads[0].wait()
     j256, k64 = iota((256, 64), 0), iota((256, 64), 1)
@@ -151,7 +145,7 @@
                     (nl[i, r] - sigma * part) / LSCALE + LSHIFT
                 ).astype(BF)
 
-    pl.semaphore_wait(bar, 45)
+    pl.semaphore_wait(bar, 39)
 
     main_pos = 1 + c
     halo_j = 2 * y + zh + 2 * c - 1
@@ -189,6 +183,34 @@
     @pl.when(j == 7)
     def _():
         rbuf[3] = jnp.zeros((64, 128), BF)
+
+    def flip(k, carry):
+        start = pl.multiple_of(k * 128, 128)
+        for h in range(2):
+            block = mod[h * 128 : h * 128 + 128, pl.ds(start, 128)]
+            modt[h, pl.ds(start, 128), :] = block.astype(F32).T.astype(BF)
+        return carry
+
+    lax.fori_loop(0, 19, flip, 0)
+    half = D // 2
+    place4 = zh * 2 + c
+    mod_lane = pl.ds(pl.multiple_of(place4 * 128, 128), 128)
+    modp[:, mod_lane] = modt[zh, pl.ds(pl.multiple_of(c * half, 64), half), :]
+    mod_copies = []
+    for d in range(1, 4):
+        n = lax.rem(place4 + d, 4)
+        h, core = lax.div(n, 2), lax.rem(n, 2)
+        for part, (low, size) in enumerate(((0, 608), (608, 608))):
+            mod_copies.append(
+                pltpu.make_async_remote_copy(
+                    src_ref=modt.at[h, pl.ds(pl.multiple_of(core * half + low, 32), size), :],
+                    dst_ref=modp.at[low : low + size, mod_lane],
+                    send_sem=mod_s.at[part, d - 1], recv_sem=mod_r.at[part, d - 1],
+                    device_id={"tok": y * 2 + h, "grp": core}, device_id_type=MESH,
+                )
+            )
+    for copy in mod_copies:
+        copy.start()
 
     for copy in loads[5:11]:
         copy.wait()
@@ -237,9 +259,9 @@
     sum_one = jnp.zeros((8, CH), F32)
     sum_two = jnp.zeros((8, CH), F32)
     for o in range(8):
-        out = mm(lhs[...], wb[:, o * CH : (o + 1) * CH]) + inb[...]
-        first[:, o] = out.reshape(14, 16, CH)
-        own = out[48:176].reshape(16, 8, CH)
+        out = mm(lhs[48:176, :], wb[:, o * CH : (o + 1) * CH]) + inb[...]
+        first[3:11, o] = out.reshape(8, 16, CH)
+        own = out.reshape(16, 8, CH)
         sum_one = sum_one + jnp.sum(own, axis=0)
         sum_two = sum_two + jnp.sum(own * own, axis=0)
 
@@ -279,33 +301,11 @@
 
     pack(p1, (sum_one, sum_two))
     ex1 = exchange(0, p1)
-
-    def flip(k, carry):
-        start = pl.multiple_of(k * 128, 128)
-        for h in range(2):
-            block = mod[h * 128 : h * 128 + 128, pl.ds(start, 128)]
-            modt[h, pl.ds(start, 128), :] = block.astype(F32).T.astype(BF)
-        return carry
-
-    lax.fori_loop(0, 19, flip, 0)
-    half = D // 2
-    place4 = zh * 2 + c
-    mod_lane = pl.ds(pl.multiple_of(place4 * 128, 128), 128)
-    mod_copies = []
-    for d in range(1, 4):
-        n = lax.rem(place4 + d, 4)
-        h, core = lax.div(n, 2), lax.rem(n, 2)
-        mod_copies.append(
-            pltpu.make_async_remote_copy(
-                src_ref=modt.at[h, pl.ds(pl.multiple_of(core * half, 64), half), :],
-                dst_ref=modp.at[:, mod_lane],
-                send_sem=mod_s.at[d - 1], recv_sem=mod_r.at[d - 1],
-                device_id={"tok": y * 2 + h, "grp": core}, device_id_type=MESH,
-            )
-        )
-    for copy in mod_copies:
-        copy.start()
-    modp[:, mod_lane] = modt[zh, pl.ds(pl.multiple_of(c * half, 64), half), :]
+    beside = jnp.concatenate([lhs[0:48, :], lhs[176:224, :]], axis=0)
+    for o in range(8):
+        out = (mm(beside, wb[:, o * CH : (o + 1) * CH]) + inb[...]).reshape(6, 16, CH)
+        first[0:3, o] = out[0:3]
+        first[11:14, o] = out[3:6]
 
     stats = group_total(collect(p1, ex1)) / GROUP_N
     mu = as_row(stats, 0)
@@ -337,7 +337,7 @@
         total = None
         for dy in range(3):
             for dx in range(3):
-                part = [act[r + dy : r + dy + n, dx : dx + 8].reshape(n * 128, CH) for r, n in pieces]
+                part = [act[pl.ds(r + dy, n), dx : dx + 8].reshape(n * 128, CH) for r, n in pieces]
                 part = part[0] if len(part) == 1 else jnp.concatenate(part, axis=0)
                 term = mm(part, midk[dy, dx])
                 total = term if total is None else total + term
@@ -346,18 +346,19 @@
         grad = 0.5 * ((1.0 + tanh) + half_u * (1.0 - tanh * tanh))
         return half_u * (1.0 + tanh), grad
 
-    pooled_sum = jnp.zeros((8, CH), F32)
-    for i in range(4):
-        r = 2 + 2 * i
-        value, grad = decode([(r, 2)])
-        slope[r : r + 2] = grad.reshape(2, 8, 16, CH)
+    def own_decode(i, total):
+        r = 2 + 4 * i
+        value, grad = decode([(r, 4)])
+        slope[pl.ds(r, 4)] = grad.reshape(4, 8, 16, CH)
         pixel = mm_nt(rgbt, value.astype(BF))
         for colour in range(3):
-            for row in range(2):
-                at = colour * 8 + 2 * i + row
-                pixg[zh, j, at : at + 1, :] = pixel[colour : colour + 1, row * 128 : row * 128 + 128]
-        pooled_sum = pooled_sum + jnp.sum(value.reshape(32, 8, CH), axis=0)
-
+            for row in range(4):
+                pixg[zh, j, pl.ds(colour * 8 + 4 * i + row, 1), :] = (
+                    pixel[colour : colour + 1, row * 128 : row * 128 + 128]
+                )
+        return total + jnp.sum(value.reshape(64, 8, CH), axis=0)
+
+    pooled_sum = lax.fori_loop(0, 2, own_decode, jnp.zeros((8, CH), F32))
     pack(p2, (pooled_sum,))
     ex2 = exchange(1, p2)
 
@@ -371,8 +372,6 @@
                 device_id={"tok": lax.div(n, 2), "grp": lax.rem(n, 2)}, device_id_type=MESH,
             )
         )
-    for copy in pix_copies:
-        copy.start()
 
     _, grad = decode([(0, 2), (10, 2)])
     slope[0:2] = grad[:256].reshape(2, 8, 16, CH)
@@ -381,6 +380,8 @@
     loads[12].wait()
     loads[13].wait()
     pooled = (as_row(collect(p2, ex2), 0) / CELLS).astype(BF)
+    for copy in pix_copies:
+        copy.start()
     feature = mm(jnp.broadcast_to(pooled, (8, CH)), clip[...])
     target = text[pl.ds(zh, 1), :]
     norm_f = jnp.sqrt(jnp.sum(feature * feature, axis=-1, keepdims=True) + EPS)
@@ -410,26 +411,30 @@
         for dy in range(3):
             for dx in range(3):
                 part = [
-                    gsec[r + 2 - dy : r + 2 - dy + n, 2 - dx : 10 - dx].reshape(n * 128, CH)
+                    gsec[pl.ds(r + 2 - dy, n), 2 - dx : 10 - dx].reshape(n * 128, CH)
                     for r, n in pieces
                 ]
                 part = part[0] if len(part) == 1 else jnp.concatenate(part, axis=0)
                 term = mm_nt(part, midk[dy, dx])
                 total = term if total is None else total + term
-        value = [first[r + 2 : r + 2 + n].reshape(n * 128, CH) for r, n in pieces]
+        value = [first[pl.ds(r + 2, n)].reshape(n * 128, CH) for r, n in pieces]
         value = value[0] if len(value) == 1 else jnp.concatenate(value, axis=0)
         half_u = value * coef_a + coef_b
         tanh = jnp.tanh(half_u)
         grad = 0.5 * ((1.0 + tanh) + half_u * (1.0 - tanh * tanh))
         return total * (grad * gain[...]), value * rstd - xh_b
 
-    sums = [jnp.zeros((8, CH), F32)] * 2
-    for i in range(4):
-        r = 1 + 2 * i
-        w, xhat = back([(r, 2)])
-        wgr[r : r + 2] = w.reshape(2, 8, 16, CH)
-        sums[0] = sums[0] + jnp.sum(w.reshape(32, 8, CH), axis=0)
-        sums[1] = sums[1] + jnp.sum((w * xhat).reshape(32, 8, CH), axis=0)
+    def own_back(i, carry):
+        r = 1 + 4 * i
+        w, xhat = back([(r, 4)])
+        wgr[pl.ds(r, 4)] = w.reshape(4, 8, 16, CH)
+        return (
+            carry[0] + jnp.sum(w.reshape(64, 8, CH), axis=0),
+            carry[1] + jnp.sum((w * xhat).reshape(64, 8, CH), axis=0),
+        )
+
+    zero = jnp.zeros((8, CH), F32)
+    sums = lax.fori_loop(0, 2, own_back, (zero, zero))
     pack(p3, sums)
     ex3 = exchange(2, p3)
     w, _ = back([(0, 1), (9, 1)])
@@ -636,7 +641,12 @@
 
 def hand_out(*refs):
     sem = refs[8]
-    copies = [pltpu.make_async_copy(refs[i], refs[4 + i], sem.at[i]) for i in range(4)]
+    pairs = [(refs[i], refs[4 + i]) for i in range(1, 4)]
+    for h in range(2):
+        for k in range(4):
+            rows = pl.ds(k * 32, 32)
+            pairs.append((refs[0].at[h, rows, :], refs[4].at[h, rows, :]))
+    copies = [pltpu.make_async_copy(src, dst, sem.at[i]) for i, (src, dst) in enumerate(pairs)]
     for copy in copies:
         copy.start()
     for copy in copies:
@@ -679,7 +689,7 @@
             v(BF, 16, 48, 128), v(BF, 16, 48, 128), v(F32, 2, 24, 128), v(F32, 8, 24, 128),
             v(BF, 256, 256),
             dma((14,)), dma((4,)), dma((4,)), dma((3, 7)), dma((3, 7)), dma((15,)), dma((15,)),
-            dma, dma, dma((3,)), dma((3,)), dma, dma, dma((2,)), dma((2,)), dma((15,)), dma((15,)), dma((8,)), dma((8,)),
+            dma, dma, dma((2, 3)), dma((2, 3)), dma, dma, dma((2,)), dma((2,)), dma((15,)), dma((15,)), dma((8,)), dma((8,)),
         ],
         compiler_params=pltpu.CompilerParams(
             collective_id=0, has_side_effects=True, vmem_limit_bytes=58 * 2**20
@@ -699,8 +709,8 @@
         ),
         in_specs=[vmem] * 4,
         out_specs=[any_spec] * 4,
-        scratch_shapes=[dma((4,))],
-    )(hg, wg, reward, pixels)
+        scratch_shapes=[dma((11,))],
+    )(*[pltpu.with_memory_space_constraint(out, pltpu.VMEM) for out in (hg, wg, reward, pixels)])
     return hg, wg, reward.reshape(2), pixels
 
 

time: 70.7 us -> 62.9 us (0.89)
  Pallas kernels: 67 us -> 62 us
  local copies, waits for them, and re-layouts: 2.76 us -> 0 us
    pallas_call x1, Pallas kernels: 64.6 us -> 60.9 us  [local(): pl.pallas_call(kernel, out_shape=(pltpu.VMEM((2, 128, D), BF), pltpu.VMEM...]
    unnamed x8 -> x0, local copies, waits for them, and re-layouts: 2.76 us -> none
    pallas_call x1, Pallas kernels: 2.39 us -> 1.13 us  [local(): pl.pallas_call(hand_out, out_shape=(jax.ShapeDtypeStruct((2, 128, D), BF)...]
where the time goes in v3:
time: 62.9 us; the launch traced here: 62.8 us
  Pallas kernels  62 us (99%)
  between operations  0.81 us (1%)
    pallas_call x1, Pallas kernels, local(): pl.pallas_call(kernel, out_shape=(pltpu.VMEM((2, 128, D), BF), pltpu.VMEM...  60.9 us

profile of v3, /device:TPU:1, one launch (start us, length us, event | category | flops | bytes accessed | tf_op | source)
XLA Modules:
  0.0 62.8 jit_solution(4848070794407725469)
XLA Ops:
  0.6 60.9 %shard_map.183 = (bf16[2,128,2432]{2,1,0:T(8,128)(2,1)S(1)}, f32[19,64]{1,0:T(8,128)S(1)}, f32[1,2]{1,0:T(1,128)S(1)}, f32[2,1,4,384]{3,2,1,0:T(4,128)S(1)}) custom-call(s32[2]{0:T(128)} %time_ref.1, s32[2]{0:T(128)} %bitcast.14, bf16[2,128,2432]{2,1,0:T(8,128)(2,1)} %hidden_h.1, f32[2,2432]{1,0:T(2,128)} %shift_h.1, f32[2,2432]{1,0:T(2,128)} %scale_h.1, ...), custom_call_target="tpu_custom_call" | custom-call | tf_op jit(solution)/shard_map/pallas_call | solution.py:668
  61.5 1.1 %shard_map.184 = (bf16[2,128,2432]{2,1,0:T(8,128)(2,1)}, f32[19,64]{1,0:T(8,128)}, f32[1,2]{1,0:T(1,128)}, f32[2,1,4,384]{3,2,1,0:T(4,128)}) custom-call(bf16[2,128,2432]{2,1,0:T(8,128)(2,1)S(1)} %get-tuple-element.12.refs_0_, f32[19,64]{1,0:T(8,128)S(1)} %get-tuple-element.13.refs_1_, f32[1,2]{1,0:T(1,128)S(1)} %get-tuple-element.14.refs_2_, ...), custom_call_target="tpu_custom_call" | custom-call | tf_op jit(solution)/shard_map/pallas_call | solution.py:702

commit v4 on v3

--- a/solution.py
+++ b/solution.py
@@ -58,7 +58,7 @@
     hgv, wg_ref, rew_out, pix_out,
     hid, shiftv, scalev, outw, noisy, ink, inb, gain, nbias, midk, midb, rgb, clip, text,
     stat_m, stat_i, mod, modt, modp, wrep, ve, nl, latsend, rbuf, lhs, wb,
-    first, act, slope, gsec, wgr, gfc, rowbuf,
+    first, act, slope, gsec, wgr, outer, rowbuf,
     p1, p2, p3, rewb, pixg, gvx, gvr, wt, s1send, s1recv, s2send, s2recv, own_tokens,
     load_sem, lat_s, lat_r, ex_s, ex_r, pix_s, pix_r, rew_s, rew_r, mod_s, mod_r,
     gx_s, gx_r, gv_s, gv_r, s1_s, s1_r, s2_s, s2_r,
@@ -273,13 +273,13 @@
 
     def exchange(phase, buf):
         copies = []
-        for d in range(1, 8):
-            n = lax.rem(j + d, 8)
+        offsets = ((2, 0), (2, 1), (1, 0), (3, 0), (1, 1), (3, 1), (0, 1))
+        for d, (dy, dc) in enumerate(offsets):
             copies.append(
                 pltpu.make_async_remote_copy(
                     src_ref=buf.at[j], dst_ref=buf.at[j],
-                    send_sem=ex_s.at[phase, d - 1], recv_sem=ex_r.at[phase, d - 1],
-                    device_id={"tok": lax.div(n, 2) * 2 + zh, "grp": lax.rem(n, 2)},
+                    send_sem=ex_s.at[phase, d], recv_sem=ex_r.at[phase, d],
+                    device_id={"tok": lax.rem(y + dy, 4) * 2 + zh, "grp": lax.rem(c + dc, 2)},
                     device_id_type=MESH,
                 )
             )
@@ -323,13 +323,12 @@
     def inside(row):
         return ((row >= 0) & (row < 64)).astype(F32)
 
-    def act_row(r, carry):
-        half_u = first[r] * coef_a + coef_b
-        value = half_u * (1.0 + jnp.tanh(half_u)) * inside(8 * j - 3 + r)
-        put_row(act, r, value)
-        return carry
-
-    lax.fori_loop(0, 14, act_row, 0)
+    def act_rows(rows):
+        for r in rows:
+            half_u = first[r] * coef_a + coef_b
+            put_row(act, r, half_u * (1.0 + jnp.tanh(half_u)) * inside(8 * j - 3 + r))
+
+    act_rows((2, 3, 4, 5))
 
     loads[11].wait()
 
@@ -337,7 +336,7 @@
         total = None
         for dy in range(3):
             for dx in range(3):
-                part = [act[pl.ds(r + dy, n), dx : dx + 8].reshape(n * 128, CH) for r, n in pieces]
+                part = [act[r + dy : r + dy + n, dx : dx + 8].reshape(n * 128, CH) for r, n in pieces]
                 part = part[0] if len(part) == 1 else jnp.concatenate(part, axis=0)
                 term = mm(part, midk[dy, dx])
                 total = term if total is None else total + term
@@ -346,19 +345,19 @@
         grad = 0.5 * ((1.0 + tanh) + half_u * (1.0 - tanh * tanh))
         return half_u * (1.0 + tanh), grad
 
-    def own_decode(i, total):
-        r = 2 + 4 * i
-        value, grad = decode([(r, 4)])
-        slope[pl.ds(r, 4)] = grad.reshape(4, 8, 16, CH)
+    pooled_sum = jnp.zeros((8, CH), F32)
+    for i in range(4):
+        r = 2 + 2 * i
+        act_rows(((6, 7), (8, 9), (10, 11), (0, 1, 12, 13))[i])
+        value, grad = decode([(r, 2)])
+        slope[r : r + 2] = grad.reshape(2, 8, 16, CH)
         pixel = mm_nt(rgbt, value.astype(BF))
         for colour in range(3):
-            for row in range(4):
-                pixg[zh, j, pl.ds(colour * 8 + 4 * i + row, 1), :] = (
-                    pixel[colour : colour + 1, row * 128 : row * 128 + 128]
-                )
-        return total + jnp.sum(value.reshape(64, 8, CH), axis=0)
-
-    pooled_sum = lax.fori_loop(0, 2, own_decode, jnp.zeros((8, CH), F32))
+            for row in range(2):
+                at = colour * 8 + 2 * i + row
+                pixg[zh, j, at : at + 1, :] = pixel[colour : colour + 1, row * 128 : row * 128 + 128]
+        pooled_sum = pooled_sum + jnp.sum(value.reshape(32, 8, CH), axis=0)
+
     pack(p2, (pooled_sum,))
     ex2 = exchange(1, p2)
 
@@ -373,6 +372,10 @@
             )
         )
 
+    for r in range(10):
+        half_u = first[r + 2] * coef_a + coef_b
+        tanh = jnp.tanh(half_u)
+        outer[r] = ((1.0 + tanh) + half_u * (1.0 - tanh * tanh)) * (gain[...] * 0.5)
     _, grad = decode([(0, 2), (10, 2)])
     slope[0:2] = grad[:256].reshape(2, 8, 16, CH)
     slope[10:12] = grad[256:].reshape(2, 8, 16, CH)
@@ -398,11 +401,11 @@
     )
     rew_copy.start()
 
-    def grad_row(r, carry):
-        put_row(gsec, r, slope[r] * grad_act * inside(8 * j - 2 + r))
-        return carry
-
-    lax.fori_loop(0, 12, grad_row, 0)
+    def grad_rows(rows):
+        for r in rows:
+            put_row(gsec, r, slope[r] * grad_act * inside(8 * j - 2 + r))
+
+    grad_rows((1, 2, 3, 4))
 
     xh_b = mu * rstd
 
@@ -411,30 +414,26 @@
         for dy in range(3):
             for dx in range(3):
                 part = [
-                    gsec[pl.ds(r + 2 - dy, n), 2 - dx : 10 - dx].reshape(n * 128, CH)
+                    gsec[r + 2 - dy : r + 2 - dy + n, 2 - dx : 10 - dx].reshape(n * 128, CH)
                     for r, n in pieces
                 ]
                 part = part[0] if len(part) == 1 else jnp.concatenate(part, axis=0)
                 term = mm_nt(part, midk[dy, dx])
                 total = term if total is None else total + term
-        value = [first[pl.ds(r + 2, n)].reshape(n * 128, CH) for r, n in pieces]
-        value = value[0] if len(value) == 1 else jnp.concatenate(value, axis=0)
-        half_u = value * coef_a + coef_b
-        tanh = jnp.tanh(half_u)
-        grad = 0.5 * ((1.0 + tanh) + half_u * (1.0 - tanh * tanh))
-        return total * (grad * gain[...]), value * rstd - xh_b
-
-    def own_back(i, carry):
-        r = 1 + 4 * i
-        w, xhat = back([(r, 4)])
-        wgr[pl.ds(r, 4)] = w.reshape(4, 8, 16, CH)
-        return (
-            carry[0] + jnp.sum(w.reshape(64, 8, CH), axis=0),
-            carry[1] + jnp.sum((w * xhat).reshape(64, 8, CH), axis=0),
-        )
-
-    zero = jnp.zeros((8, CH), F32)
-    sums = lax.fori_loop(0, 2, own_back, (zero, zero))
+        def rows_of(buf, shift):
+            part = [buf[r + shift : r + shift + n].reshape(n * 128, CH) for r, n in pieces]
+            return part[0] if len(part) == 1 else jnp.concatenate(part, axis=0)
+
+        return total * rows_of(outer, 0), rows_of(first, 2) * rstd - xh_b
+
+    sums = [jnp.zeros((8, CH), F32)] * 2
+    for i in range(4):
+        r = 1 + 2 * i
+        grad_rows(((5, 6), (7, 8), (9, 10), (0, 11))[i])
+        w, xhat = back([(r, 2)])
+        wgr[r : r + 2] = w.reshape(2, 8, 16, CH)
+        sums[0] = sums[0] + jnp.sum(w.reshape(32, 8, CH), axis=0)
+        sums[1] = sums[1] + jnp.sum((w * xhat).reshape(32, 8, CH), axis=0)
     pack(p3, sums)
     ex3 = exchange(2, p3)
     w, _ = back([(0, 1), (9, 1)])
@@ -447,16 +446,14 @@
     coef_f = -rstd * rstd * mean_x
     coef_0 = (xh_b * mean_x - mean_w) * rstd
 
-    def first_row(r, carry):
-        value = wgr[r] * rstd + first[r + 2] * coef_f + coef_0
-        value = (value * inside(8 * j - 1 + r)).astype(BF)
-        start = pl.multiple_of(r * 16, 16)
-        for o in range(8):
-            gfc[pl.ds(start, 16), o * CH : (o + 1) * CH] = value[o]
-        return carry
-
-    lax.fori_loop(0, 10, first_row, 0)
-    back_y = mm_nt(gfc[...], wb[...])
+    row = 8 * j - 1 + (iota((160, 1), 0) >> 4)
+    keep_row = ((row >= 0) & (row < 64)).astype(F32)
+    back_y = None
+    for o in range(8):
+        value = wgr[:, o].reshape(160, CH) * rstd + first[2:12, o].reshape(160, CH) * coef_f
+        value = ((value + coef_0) * keep_row).astype(BF)
+        term = mm_nt(value, wb[:, o * CH : (o + 1) * CH])
+        back_y = term if back_y is None else back_y + term
     grad_lat = jnp.zeros((128, 128), F32)
     edge = jnp.zeros((128, 128), F32)
     lane = iota((128, 128), 1)
@@ -525,14 +522,15 @@
         s1send[k, 32:48, :] = tail.astype(BF)
     me_xy = x * 4 + y
     s1 = []
-    for d in range(1, 16):
-        n = lax.rem(me_xy + d, 16)
+    offsets = [(dx, dy) for dx in range(4) for dy in range(4) if dx or dy]
+    offsets.sort(key=lambda o: -min(o[0], 4 - o[0]) - min(o[1], 4 - o[1]))
+    for d, (dx, dy) in enumerate(offsets):
+        to_x, to_y = lax.rem(x + dx, 4), lax.rem(y + dy, 4)
         s1.append(
             pltpu.make_async_remote_copy(
-                src_ref=s1send.at[n], dst_ref=s1recv.at[me_xy],
-                send_sem=s1_s.at[d - 1], recv_sem=s1_r.at[d - 1],
-                device_id={"batch": zl * 4 + lax.div(n, 4), "tok": lax.rem(n, 4) * 2 + zh},
-                device_id_type=MESH,
+                src_ref=s1send.at[to_x * 4 + to_y], dst_ref=s1recv.at[me_xy],
+                send_sem=s1_s.at[d], recv_sem=s1_r.at[d],
+                device_id={"batch": zl * 4 + to_x, "tok": to_y * 2 + zh}, device_id_type=MESH,
             )
         )
     for copy in s1:
@@ -683,7 +681,7 @@
             v(BF, 256, D), v(F32, 2, 256, 128), v(F32, 2, 4, 16, 128), v(BF, 2, 64, 128),
             v(BF, 4, 64, 128), v(BF, 224, 512), v(BF, 512, 8 * CH),
             v(F32, 14, 8, 16, CH), v(BF, 14, 10, 16, CH), v(F32, 12, 8, 16, CH),
-            v(BF, 12, 10, 16, CH), v(F32, 10, 8, 16, CH), v(BF, 160, 8 * CH), v(F32, 8, 128),
+            v(BF, 12, 10, 16, CH), v(F32, 10, 8, 16, CH), v(F32, 10, 8, 16, CH), v(F32, 8, 128),
             v(F32, 8, 8, 128), v(F32, 8, 8, 128), v(F32, 8, 8, 128), v(F32, 2, 8, 128),
             v(F32, 2, 8, 24, 128), v(BF, 2, 2, 64, 128), v(BF, 2, 64, 128), v(F32, 608, 128),
             v(BF, 16, 48, 128), v(BF, 16, 48, 128), v(F32, 2, 24, 128), v(F32, 8, 24, 128),

time: 62.9 us -> 61.8 us (0.983)
  Pallas kernels: 62 us -> 60.6 us
    pallas_call x1, Pallas kernels: 60.9 us -> 59.5 us  [local(): pl.pallas_call(kernel, out_shape=(pltpu.VMEM((2, 128, D), BF), pltpu.VMEM...]
where the time goes in v4:
time: 61.8 us; the launch traced here: 61.4 us
  Pallas kernels  60.6 us (98%)
  between operations  0.81 us (1%)
    pallas_call x1, Pallas kernels, local(): pl.pallas_call(kernel, out_shape=(pltpu.VMEM((2, 128, D), BF), pltpu.VMEM...  59.5 us

profile of v4, /device:TPU:1, one launch (start us, length us, event | category | flops | bytes accessed | tf_op | source)
XLA Modules:
  0.0 61.4 jit_solution(5911923344245402225)
XLA Ops:
  0.6 59.5 %shard_map.183 = (bf16[2,128,2432]{2,1,0:T(8,128)(2,1)S(1)}, f32[19,64]{1,0:T(8,128)S(1)}, f32[1,2]{1,0:T(1,128)S(1)}, f32[2,1,4,384]{3,2,1,0:T(4,128)S(1)}) custom-call(s32[2]{0:T(128)} %time_ref.1, s32[2]{0:T(128)} %bitcast.14, bf16[2,128,2432]{2,1,0:T(8,128)(2,1)} %hidden_h.1, f32[2,2432]{1,0:T(2,128)} %shift_h.1, f32[2,2432]{1,0:T(2,128)} %scale_h.1, ...), custom_call_target="tpu_custom_call" | custom-call | tf_op jit(solution)/shard_map/pallas_call | solution.py:666
  60.1 1.1 %shard_map.184 = (bf16[2,128,2432]{2,1,0:T(8,128)(2,1)}, f32[19,64]{1,0:T(8,128)}, f32[1,2]{1,0:T(1,128)}, f32[2,1,4,384]{3,2,1,0:T(4,128)}) custom-call(bf16[2,128,2432]{2,1,0:T(8,128)(2,1)S(1)} %get-tuple-element.12.refs_0_, f32[19,64]{1,0:T(8,128)S(1)} %get-tuple-element.13.refs_1_, f32[1,2]{1,0:T(1,128)S(1)} %get-tuple-element.14.refs_2_, ...), custom_call_target="tpu_custom_call" | custom-call | tf_op jit(solution)/shard_map/pallas_call | solution.py:700

commit v5 on v4

--- a/solution.py
+++ b/solution.py
@@ -382,13 +382,11 @@
 
     loads[12].wait()
     loads[13].wait()
+    target = text[pl.ds(zh, 1), :]
+    norm_t = jnp.sqrt(jnp.sum(target * target, axis=-1, keepdims=True) + EPS)
     pooled = (as_row(collect(p2, ex2), 0) / CELLS).astype(BF)
-    for copy in pix_copies:
-        copy.start()
     feature = mm(jnp.broadcast_to(pooled, (8, CH)), clip[...])
-    target = text[pl.ds(zh, 1), :]
     norm_f = jnp.sqrt(jnp.sum(feature * feature, axis=-1, keepdims=True) + EPS)
-    norm_t = jnp.sqrt(jnp.sum(target * target, axis=-1, keepdims=True) + EPS)
     reward = jnp.sum(feature * target, axis=-1, keepdims=True) / (norm_f * norm_t)
     grad_feature = (
         REWARD_W * (target / (norm_f * norm_t) - reward * feature / (norm_f * norm_f))
@@ -431,6 +429,8 @@
         r = 1 + 2 * i
         grad_rows(((5, 6), (7, 8), (9, 10), (0, 11))[i])
         w, xhat = back([(r, 2)])
+        for copy in pix_copies[4 * i : 4 * i + 4]:
+            copy.start()
         wgr[r : r + 2] = w.reshape(2, 8, 16, CH)
         sums[0] = sums[0] + jnp.sum(w.reshape(32, 8, CH), axis=0)
         sums[1] = sums[1] + jnp.sum((w * xhat).reshape(32, 8, CH), axis=0)
@@ -610,20 +610,6 @@
     lane = iota((1, 128), 1)
     rew_out[...] = jnp.where(lane == 0, rewb[0, 0:1, :], rewb[1, 0:1, :])[:, 0:2]
 
-    for n in range(8):
-        copy = pltpu.make_async_remote_copy(
-            src_ref=s2send.at[0], dst_ref=s2recv.at[n],
-            send_sem=s2_s.at[0], recv_sem=s2_r.at[n],
-            device_id={"grp": 1 - c}, device_id_type=MESH,
-        )
-        pl.when(jnp.logical_not(self_line & (me_z == n)))(copy.wait_recv)
-    total = s2recv[0]
-    for k in range(1, 8):
-        total = total + s2recv[k]
-    odd = jnp.full((24, 128), lax.rem(zl, 2), jnp.int32) == 1
-    total = jnp.where(odd, pltpu.roll(total, 64, 1), total)
-    wg_ref[...] = total[0:19, 0:64]
-
     for h in range(2):
         for copy, ok in lat_copies(h):
             pl.when(ok)(copy.wait_send)
@@ -632,6 +618,20 @@
     for e in range(2):
         copy, ok = gv_copy(e)
         pl.when(ok)(copy.wait_send)
+    for n in range(8):
+        copy = pltpu.make_async_remote_copy(
+            src_ref=s2send.at[0], dst_ref=s2recv.at[n],
+            send_sem=s2_s.at[0], recv_sem=s2_r.at[n],
+            device_id={"grp": 1 - c}, device_id_type=MESH,
+        )
+        pl.when(jnp.logical_not(self_line & (me_z == n)))(copy.wait_recv)
+    total = s2recv[0]
+    for k in range(1, 8):
+        total = total + s2recv[k]
+    odd = jnp.full((24, 128), lax.rem(zl, 2), jnp.int32) == 1
+    total = jnp.where(odd, pltpu.roll(total, 64, 1), total)
+    wg_ref[...] = total[0:19, 0:64]
+
     for n in range(8):
         copy, ok = line_copy(n)
         pl.when(ok)(copy.wait_send)

time: 61.8 us -> 61.7 us (level)
  no operation moved by 1% of the time
where the time goes in v5:
time: 61.7 us; the launch traced here: 61.3 us
  Pallas kernels  60.5 us (98%)
  between operations  0.81 us (1%)
    pallas_call x1, Pallas kernels, local(): pl.pallas_call(kernel, out_shape=(pltpu.VMEM((2, 128, D), BF), pltpu.VMEM...  59.4 us

profile of v5, /device:TPU:1, one launch (start us, length us, event | category | flops | bytes accessed | tf_op | source)
XLA Modules:
  0.0 61.3 jit_solution(16878141432338015308)
XLA Ops:
  0.6 59.4 %shard_map.183 = (bf16[2,128,2432]{2,1,0:T(8,128)(2,1)S(1)}, f32[19,64]{1,0:T(8,128)S(1)}, f32[1,2]{1,0:T(1,128)S(1)}, f32[2,1,4,384]{3,2,1,0:T(4,128)S(1)}) custom-call(s32[2]{0:T(128)} %time_ref.1, s32[2]{0:T(128)} %bitcast.14, bf16[2,128,2432]{2,1,0:T(8,128)(2,1)} %hidden_h.1, f32[2,2432]{1,0:T(2,128)} %shift_h.1, f32[2,2432]{1,0:T(2,128)} %scale_h.1, ...), custom_call_target="tpu_custom_call" | custom-call | tf_op jit(solution)/shard_map/pallas_call | solution.py:666
  60.0 1.1 %shard_map.184 = (bf16[2,128,2432]{2,1,0:T(8,128)(2,1)}, f32[19,64]{1,0:T(8,128)}, f32[1,2]{1,0:T(1,128)}, f32[2,1,4,384]{3,2,1,0:T(4,128)}) custom-call(bf16[2,128,2432]{2,1,0:T(8,128)(2,1)S(1)} %get-tuple-element.12.refs_0_, f32[19,64]{1,0:T(8,128)S(1)} %get-tuple-element.13.refs_1_, f32[1,2]{1,0:T(1,128)S(1)} %get-tuple-element.14.refs_2_, ...), custom_call_target="tpu_custom_call" | custom-call | tf_op jit(solution)/shard_map/pallas_call | solution.py:700
